TPU v7x, 32 devices: a whole 2x2x4 slice. The times are simulated.
32 devices in a mesh: section: 2 (over core), dp: 16 (over z, y, x).
Axes of the slice: x: 2, y: 2, z: 4, core: 2. Of those that a mesh axis runs over, the one named last changes fastest.
Arguments:
- inputs: bfloat16 [32, 1024, 768], P('dp'), may hold values from -6 to 6
- cotangent: bfloat16 [32, 1024, 768], P('dp'), may hold values from -6 to 6
- lengths: int32 [32], replicated, may hold values from 64 to 1024, as said below
- assignment: int32 [32], P('dp'), may hold values from 0 to 31, each once
- skip_flags: int32 [2, 2], P(None, 'section'), may hold values from 0 to 1, as said below
- head_counts: int32 [2, 2], P(None, 'section'), may hold values from 8 to 12, as said below
- ffn_counts: int32 [2, 2], P(None, 'section'), may hold values from 1920 to 3072, as said below
- w_qkv: bfloat16 [2, 768, 2304], P('section'), may hold values from -0.21875 to 0.21875
- bias_q: bfloat16 [2, 768], P('section'), may hold values from -1 to 1
- bias_v: bfloat16 [2, 768], P('section'), may hold values from -1 to 1
- w_out: bfloat16 [2, 768, 768], P('section'), may hold values from -0.875 to 0.875
- bias_out: bfloat16 [2, 768], P('section'), may hold values from -1 to 1
- norm1_gain: bfloat16 [2, 768], P('section'), may hold values from 0.5 to 1.5
- norm1_bias: bfloat16 [2, 768], P('section'), may hold values from -1 to 1
- w_up: bfloat16 [2, 768, 3072], P('section'), may hold values from -0.21875 to 0.21875
- bias_up: bfloat16 [2, 3072], P('section'), may hold values from -1 to 1
- w_down: bfloat16 [2, 3072, 768], P('section'), may hold values from -0.109375 to 0.109375
- bias_down: bfloat16 [2, 768], P('section'), may hold values from -1 to 1
- norm2_gain: bfloat16 [2, 768], P('section'), may hold values from 0.5 to 1.5
- norm2_bias: bfloat16 [2, 768], P('section'), may hold values from -1 to 1
Outputs:
- output: float32 [32, 1024, 768], P('dp', None, 'section')
- input_grad: float32 [32, 1024, 768], P('dp', None, 'section')
- grad_w_qkv: float32 [2, 768, 2304], P('section')
- grad_bias_q: float32 [2, 768], P('section')
- grad_bias_v: float32 [2, 768], P('section')
- grad_w_out: float32 [2, 768, 768], P('section')
- grad_bias_out: float32 [2, 768], P('section')
- grad_norm1_gain: float32 [2, 768], P('section')
- grad_norm1_bias: float32 [2, 768], P('section')
- grad_w_up: float32 [2, 768, 3072], P('section')
- grad_bias_up: float32 [2, 3072], P('section')
- grad_w_down: float32 [2, 3072, 768], P('section')
- grad_bias_down: float32 [2, 768], P('section')
- grad_norm2_gain: float32 [2, 768], P('section')
- grad_norm2_bias: float32 [2, 768], P('section')
Inputs may be any that keep to these rules, and one draw needn't show every extreme that they name: `lengths`: some utterance has 1024 frames and some has the least. `skip_flags`: each micro-batch skips at most one layer; some micro-batch skips one. `head_counts`: in each micro-batch one layer has all 12 heads and the other 12 - 2k heads with k 1 or 2; k is 2 in some micro-batch. `ffn_counts`: in each micro-batch one layer has all 3072 units and the other 3072 - k * (96) with k from 1 to 12; k is 12 in some micro-batch.
All inputs are finite; a program needn't handle non-finite values.
Results may differ from a plain program's by a relative error of at most 0.014.
Values may be sent and summed in bfloat16 or wider, within the bound.
No kernel may reach another device: no remote copies, remote signals or barrier semaphores. Data moves between devices by JAX's collectives and lax.ppermute only.
A program may use at most 576 MiB of HBM per device.

v0:
```python
import functools

import jax
import jax.numpy as jnp
from jax import lax
from jax.experimental import pallas as pl
from jax.experimental.pallas import tpu as pltpu
from jax.sharding import PartitionSpec as P

HEADS = 12
MICRO = 2
NORM_EPS = 1e-05
NEG_FILL = -1e30
F32 = jnp.float32
BF16 = jnp.bfloat16

ROWS = 256
UNITS = 512
LEAST = 1920 // UNITS
SAFE = 40.0
VMEM_BYTES = 64 * 1024 * 1024

OWN, BLOCKS, LIVE, LENGTH, PAIRS, COUNT, CHUNKS, SLOT, SKIP, SECTION = range(10)
V_BQ, V_ZERO, V_BV, V_BO, V_G1, V_B1, V_BU, V_BD, V_G2, V_B2 = 0, 1, 2, 3, 4, 5, 6, 10, 11, 12


def dot(left, right):
    return lax.dot_general(left, right, (((1,), (0,)), ((), ())), preferred_element_type=F32)


def dot_nt(left, right):
    return lax.dot_general(left, right, (((1,), (1,)), ((), ())), preferred_element_type=F32)


def dot_tn(left, right):
    return lax.dot_general(left, right, (((0,), (0,)), ((), ())), preferred_element_type=F32)


def rows_at(block):
    if isinstance(block, int):
        return pl.ds(block * ROWS, ROWS)
    return pl.ds(pl.multiple_of(block * ROWS, ROWS), ROWS)


def cols_at(start, size):
    if isinstance(start, int):
        return pl.ds(start, size)
    return pl.ds(pl.multiple_of(start, 128), size)


def facts(layer, own_counts, other_counts, assigned, lengths):
    section = lax.axis_index("section")
    own = section == layer

    def count(row):
        at = row * MICRO + section
        return jnp.where(own, own_counts[at], other_counts[at])

    skip, heads, units = count(0), count(1), count(2)
    length = lengths[assigned[section]]
    live = (length + ROWS - 1) // ROWS
    blocks = jnp.where(skip == 1, 0, live)
    chunks = jnp.where(skip == 1, 0, (units + UNITS - 1) // UNITS)
    return [own.astype(jnp.int32), blocks, live, length, heads // 2, units, chunks, section, skip, section]


def by_blocks(count, most, body):
    for blocks in range(2, most + 1, 2):
        pl.when((count == blocks) | (count == blocks - 1))(functools.partial(body, blocks))


def clear_odd(count, *refs):
    @pl.when(count % 2 == 1)
    def _():
        for ref in refs:
            ref[rows_at(count), :] = jnp.zeros((ROWS, ref.shape[1]), ref.dtype)


def by_chunks(count, most, body):
    body(0, LEAST + 1)
    pl.when(count > LEAST + 1)(functools.partial(body, LEAST + 1, most))


def fetch_start(s, dst, own_ref, other_ref, sem):
    @pl.when(s[OWN] == 1)
    def _():
        pltpu.make_async_copy(own_ref, dst, sem).start()

    @pl.when(s[OWN] == 0)
    def _():
        pltpu.make_async_copy(other_ref, dst, sem).start()


def live_column(s, block):
    frame = lax.broadcasted_iota(jnp.int32, (ROWS, 1), 0) + block * ROWS
    return frame < s[LENGTH]


def gelu_parts(values):
    under = 1.0 + 0.2316419 * jnp.abs(values)
    t = pl.reciprocal(under, approx=True)
    t = t * (2.0 - under * t)
    poly = t * (
        0.319381530 + t * (-0.356563782 + t * (1.781477937 + t * (-1.821255978 + t * 1.330274429)))
    )
    bell = jnp.exp2(values * values * -0.7213475204444817) * 0.3989422804014327
    tail = poly * bell
    below = jnp.where(values >= 0, 1.0 - tail, tail)
    return values * below, below + values * bell


def spread_heads(width):
    head = lax.broadcasted_iota(jnp.int32, (128, width), 1) // 64
    return (head == lax.broadcasted_iota(jnp.int32, (128, width), 0)).astype(BF16)


def norm_parts(values):
    center = jnp.mean(values, axis=-1, keepdims=True)
    shifted = values - center
    spread = jnp.mean(shifted * shifted, axis=-1, keepdims=True)
    inverse = lax.rsqrt(spread + NORM_EPS)
    return shifted * inverse, inverse


def vec_row(vec_ref, row):
    return vec_ref[row : row + 1, :].astype(F32)


def forward_kernel(
    last,
    phase,
    own_counts, other_counts, assigned, lengths,
    x_hbm,
    wq0, wq1, wo0, wo1, wu0, wu1, wd0, wd1, v0, v1,
    *rest,
):
    s = facts(1 if last else 0, own_counts, other_counts, assigned, lengths)
    attends, finishes = phase != "finish", phase != "attend"
    if not attends:
        ctx_in, stat_in = rest[:2]
        rest = rest[2:]
    if finishes and last:
        keep_hbm, send_hbm = rest[:2]
        rest = rest[2:]
    elif finishes:
        pass_hbm = rest[0]
        rest = rest[1:]
    if attends:
        proj_hbm, ctx_hbm, lse_hbm = rest[:3]
        rest = rest[3:]
    if finishes:
        stat_hbm, gated_hbm, slope_hbm, x1_hbm, x2_hbm = rest[:5]
        rest = rest[5:]
    (
        h, wq, wo, wu, wd, vec, proj, ctx, stat, gated, slope, x1, x2, acc, normed_b, bias_up, largest, out_a, out_b,
        in_sem, w_sem, out_sem,
    ) = rest
    most = h.shape[0] // ROWS
    width = h.shape[1]
    pairs_all = width // 128
    blocks = s[BLOCKS]
    live = s[LIVE]
    lane = lax.broadcasted_iota(jnp.int32, (1, 128), 1)
    low = lane < 64

    def source(block):
        if last:
            return x_hbm.at[rows_at(block)]
        return x_hbm.at[s[SLOT], rows_at(block)]

    def h_copy(block):
        return pltpu.make_async_copy(source(block), h.at[rows_at(block)], in_sem.at[block])

    for block in range(most):
        pl.when(block < live)(lambda block=block: h_copy(block).start())

    @pl.when(blocks > 0)
    def _():
        fetch_start(s, vec, v0, v1, w_sem.at[0])
        if attends:
            fetch_start(s, wq, wq0, wq1, w_sem.at[1])
        if finishes:
            fetch_start(s, wo, wo0, wo1, w_sem.at[2])
            fetch_start(s, wu, wu0, wu1, w_sem.at[3])
            fetch_start(s, wd, wd0, wd1, w_sem.at[4])

    def reload(what, block):
        target, source = ((ctx, ctx_in), (stat, stat_in))[what]
        return pltpu.make_async_copy(
            source.at[rows_at(block)], target.at[rows_at(block)], out_sem.at[what, block]
        )

    if not attends:
        for block in range(most):
            @pl.when(block < blocks)
            def _(block=block):
                reload(0, block).start()
                reload(1, block).start()

    for block in range(most):
        pl.when(block < live)(lambda block=block: h_copy(block).wait())

    def save(what, source_ref, target_ref, block):
        return pltpu.make_async_copy(
            source_ref.at[rows_at(block)], target_ref.at[rows_at(block)], out_sem.at[what, block]
        )

    def emit(block, value):
        if last:
            half = width // 2
            first = s[SECTION] == 0
            out_a[rows_at(block), :] = jnp.where(first, value[:, :half], value[:, half:])
            out_b[rows_at(block), :] = jnp.where(first, value[:, half:], value[:, :half]).astype(BF16)
            save(7, out_a, keep_hbm, block).start()
            save(8, out_b, send_hbm.at[0], block).start()
        else:
            out_b[rows_at(block), :] = value.astype(BF16)
            save(7, out_b, pass_hbm, block).start()

    def attention():
        pltpu.make_async_copy(wq0, wq, w_sem.at[1]).wait()

        spread = spread_heads(width)
        largest[...] = jnp.zeros(largest.shape, F32)

        def project(block, carry):
            rows = rows_at(block)
            for part, row in ((0, V_BQ), (1, V_ZERO), (2, V_BV)):
                cols = slice(part * width, (part + 1) * width)
                proj[rows, cols] = (dot(h[rows, :], wq[:, cols]) + vec_row(vec, row)).astype(BF16)
            save(0, proj, proj_hbm, block).start()
            for part in range(2):
                value = proj[rows, part * width : (part + 1) * width].astype(F32)
                squares = dot_nt(spread, (value * value).astype(BF16))
                largest[part] = jnp.maximum(largest[part], squares)
            stat[rows, :] = jnp.zeros((ROWS, 128), F32)
            return carry

        lax.fori_loop(0, blocks, project, 0)

        clear_odd(blocks, proj)
        for pair in range(pairs_all):
            @pl.when(pair >= s[PAIRS])
            def _(pair=pair):
                ctx[:, pair * 128 : (pair + 1) * 128] = jnp.zeros((h.shape[0], 128), BF16)

        bound = jnp.max(largest[0]) * jnp.max(largest[1]) * 1.02
        safe = bound <= (SAFE * 8.0) ** 2

        def attend_safe(count):
            key_at = lax.broadcasted_iota(jnp.int32, (1, ROWS), 1)
            fills = [
                jnp.where(key_at + part * ROWS < s[LENGTH], 0.0, NEG_FILL) for part in range(count)
            ]

            span = count * ROWS

            def one(pair, carry):
                cols = cols_at(pair * 128, 128)
                q = proj[0:span, cols] * jnp.asarray(0.125, BF16)
                zero = jnp.zeros_like(q)
                ones = jnp.ones((ROWS, 128), BF16)
                q_own = [jnp.where(own, q, zero) for own in (low, ~low)]
                found = [None, None]
                for part in range(count):
                    keys = slice(part * ROWS, (part + 1) * ROWS)
                    k = proj[keys, cols_at(width + pair * 128, 128)]
                    v = proj[keys, cols_at(2 * width + pair * 128, 128)]
                    for head, own in enumerate((low, ~low)):
                        scores = dot_nt(q_own[head], k)
                        if part >= count - 2:
                            scores = scores + fills[part]
                        exps = jnp.exp(scores).astype(BF16)
                        more = dot(exps, jnp.where(own, v, ones))
                        found[head] = more if part == 0 else found[head] + more
                above = jnp.where(low, found[0], found[1])
                total = pltpu.roll(jnp.where(low, found[1], found[0]), 64, 1)
                ctx[0:span, cols] = (above / total).astype(BF16)
                logs = jnp.log(total)
                kept = stat[0:span, :]
                kept = jnp.where(lane == 2 * pair, logs[:, 0:1], kept)
                kept = jnp.where(lane == 2 * pair + 1, logs[:, 64:65], kept)
                stat[0:span, :] = kept
                return carry

            lax.fori_loop(0, s[PAIRS], one, 0)

        def attend():
            span = most * ROWS
            key_live = lax.broadcasted_iota(jnp.int32, (1, span), 1) < s[LENGTH]

            def clear_rows(block, carry):
                proj[rows_at(block), width:] = jnp.zeros((ROWS, 2 * width), BF16)
                return carry

            lax.fori_loop(blocks, most, clear_rows, 0)

            def one(step, carry):
                pair, block = step // blocks, step % blocks
                rows = rows_at(block)
                cols = cols_at(pair * 128, 128)
                q = proj[rows, cols] * jnp.asarray(0.125, BF16)
                k = proj[:, cols_at(width + pair * 128, 128)]
                v = proj[:, cols_at(2 * width + pair * 128, 128)]
                zero = jnp.zeros_like(q)
                ones = jnp.ones_like(v)
                found, peaks = [], []
                for own in (low, ~low):
                    scores = jnp.where(key_live, dot_nt(jnp.where(own, q, zero), k), NEG_FILL)
                    peak = jnp.max(scores, axis=-1, keepdims=True)
                    exps = jnp.exp(scores - peak).astype(BF16)
                    found.append(dot(exps, jnp.where(own, v, ones)))
                    peaks.append(peak)
                above = jnp.where(low, found[0], found[1])
                total = pltpu.roll(jnp.where(low, found[1], found[0]), 64, 1)
                ctx[rows, cols] = (above / total).astype(BF16)
                logs = jnp.where(low, peaks[0], peaks[1]) + jnp.log(total)
                kept = stat[rows, :]
                kept = jnp.where(lane == 2 * pair, logs[:, 0:1], kept)
                kept = jnp.where(lane == 2 * pair + 1, logs[:, 64:65], kept)
                stat[rows, :] = kept
                return carry

            lax.fori_loop(0, s[PAIRS] * blocks, one, 0)

        by_blocks(jnp.where(safe, blocks, 0), most, attend_safe)
        pl.when(jnp.logical_not(safe))(attend)

    def feed_forward():
        for piece in range(wu.shape[1] // width):
            bias_up[0:1, piece * width : (piece + 1) * width] = vec_row(vec, V_BU + piece)
        pltpu.make_async_copy(wo0, wo, w_sem.at[2]).wait()
        pltpu.make_async_copy(wu0, wu, w_sem.at[3]).wait()
        pltpu.make_async_copy(wd0, wd, w_sem.at[4]).wait()

        def finish(block, carry):
            rows = rows_at(block)
            if attends:
                save(1, ctx, ctx_hbm, block).start()
            else:
                reload(0, block).wait()
                reload(1, block).wait()
            res = h[rows, :].astype(F32) + dot(ctx[rows, :], wo[...]) + vec_row(vec, V_BO)
            hat, inverse_one = norm_parts(res)
            x1[rows, :] = hat.astype(BF16)
            save(5, x1, x1_hbm, block).start()
            normed = hat * vec_row(vec, V_G1) + vec_row(vec, V_B1)
            normed_b[...] = normed.astype(BF16)
            acc[...] = normed + vec_row(vec, V_BD)

            def units(start, stop):
                def lift(c):
                    cols = slice(c * UNITS, (c + 1) * UNITS)
                    return dot(normed_b[...], wu[:, cols]) + bias_up[0:1, cols]

                more = None
                later = lift(start)
                for c in range(start, stop):
                    cols = slice(c * UNITS, (c + 1) * UNITS)
                    lifted = later
                    if c + 1 < stop:
                        later = lift(c + 1)
                    value, grad = gelu_parts(lifted)
                    if c >= LEAST:
                        unit = lax.broadcasted_iota(jnp.int32, (1, UNITS), 1) + c * UNITS
                        value = jnp.where(unit < s[COUNT], value, 0.0)
                        grad = jnp.where(unit < s[COUNT], grad, 0.0)
                    value_b = value.astype(BF16)
                    gated[rows, cols] = value_b
                    slope[rows, cols] = grad.astype(BF16)
                    part = dot(value_b, wd[cols, :])
                    more = part if more is None else more + part
                acc[...] += more

            units(0, wu.shape[1] // UNITS)
            save(3, gated, gated_hbm, block).start()
            save(4, slope, slope_hbm, block).start()
            hat_two, inverse_two = norm_parts(acc[...])
            x2[rows, :] = hat_two.astype(BF16)
            save(6, x2, x2_hbm, block).start()
            kept = stat[rows, :]
            kept = jnp.where(lane == HEADS, inverse_one, kept)
            stat[rows, :] = jnp.where(lane == HEADS + 1, inverse_two, kept)
            save(2, stat, stat_hbm, block).start()
            result = hat_two * vec_row(vec, V_G2) + vec_row(vec, V_B2)
            emit(block, jnp.where(live_column(s, block), result, 0.0))
            return carry

        lax.fori_loop(0, blocks, finish, 0)

    @pl.when(blocks > 0)
    def _():
        pltpu.make_async_copy(v0, vec, w_sem.at[0]).wait()
        if attends:
            attention()
        if finishes:
            feed_forward()

    if not finishes:
        def keep(block, carry):
            save(1, ctx, ctx_hbm, block).start()
            save(2, stat, lse_hbm, block).start()
            return carry

        lax.fori_loop(0, blocks, keep, 0)
        for block in range(most):
            @pl.when(block < blocks)
            def _(block=block):
                save(0, proj, proj_hbm, block).wait()
                save(1, ctx, ctx_hbm, block).wait()
                save(2, stat, lse_hbm, block).wait()
        return

    @pl.when(s[SKIP] == 1)
    def _():
        def carry_on(block, carry):
            value = h[rows_at(block), :].astype(F32)
            emit(block, jnp.where(live_column(s, block), value, 0.0) if last else value)
            return carry

        lax.fori_loop(0, live, carry_on, 0)

    if last:
        def clear(block, carry):
            emit(block, jnp.zeros((ROWS, width), F32))
            return carry

        lax.fori_loop(live, most, clear, 0)

    for block in range(most):
        @pl.when(block < blocks)
        def _(block=block):
            if attends:
                save(0, proj, proj_hbm, block).wait()
                save(1, ctx, ctx_hbm, block).wait()
            save(2, stat, stat_hbm, block).wait()
            save(3, gated, gated_hbm, block).wait()
            save(4, slope, slope_hbm, block).wait()
            save(5, x1, x1_hbm, block).wait()
            save(6, x2, x2_hbm, block).wait()

        if last:
            save(7, out_a, keep_hbm, block).wait()
            save(8, out_b, send_hbm.at[0], block).wait()
        else:
            pl.when(block < live)(lambda block=block: save(7, out_b, pass_hbm, block).wait())


HBM = pl.BlockSpec(memory_space=pltpu.HBM)
SMEM = pl.BlockSpec(memory_space=pltpu.SMEM)


def layer_forward(last, phase, scalars, x, weights, attended=()):
    length, width = x.shape[-2:]
    units = weights[4].shape[1]
    blocks = length // ROWS
    shape = jax.ShapeDtypeStruct
    attends, finishes = phase != "finish", phase != "attend"
    outs = []
    if finishes and last:
        outs += [shape((length, width // 2), F32), shape((2, length, width // 2), BF16)]
    elif finishes:
        outs += [shape((length, width), BF16)]
    if attends:
        outs += [
            shape((length, 3 * width), BF16),
            shape((length, width), BF16),
            shape((length, 128), F32),
        ]
    if finishes:
        outs += [
            shape((length, 128), F32),
            shape((length, units), BF16),
            shape((length, units), BF16),
            shape((length, width), BF16),
            shape((length, width), BF16),
        ]

    def held(used, size, dtype=BF16):
        return pltpu.VMEM(size if used else (16, 128), dtype)

    return pl.pallas_call(
        functools.partial(forward_kernel, last, phase),
        out_shape=outs,
        in_specs=[SMEM] * 4 + [HBM] * (11 + len(attended)),
        out_specs=[HBM] * len(outs),
        scratch_shapes=[
            pltpu.VMEM((length, width), BF16),
            held(attends, (width, 3 * width)),
            held(finishes, (width, width)),
            held(True, (width, units)),
            held(finishes, (units, width)),
            pltpu.VMEM(weights[8].shape, BF16),
            held(attends, (length, 3 * width)),
            pltpu.VMEM((length, width), BF16),
            pltpu.VMEM((length, 128), F32),
            held(finishes, (length, units)),
            held(finishes, (length, units)),
            held(finishes, (length, width)),
            held(finishes, (length, width)),
            held(finishes, (ROWS, width), F32),
            held(finishes, (ROWS, width)),
            pltpu.VMEM((8, units), F32),
            pltpu.VMEM((2, 128, ROWS), F32),
            held(finishes and last, (length, width // 2), F32),
            held(finishes, (length, width // 2 if last else width)),
            pltpu.SemaphoreType.DMA((blocks,)),
            pltpu.SemaphoreType.DMA((5,)),
            pltpu.SemaphoreType.DMA((9, blocks)),
        ],
        compiler_params=pltpu.CompilerParams(vmem_limit_bytes=VMEM_BYTES),
        cost_estimate=pl.CostEstimate(
            flops=60_000_000_000 if phase == "attend" else 10_000_000_000,
            bytes_accessed=0,
            transcendentals=0,
        ),
        name="layer_forward_" + phase,
    )(*scalars, x, *weights, *attended)


def ffn_back_kernel(
    first_pass,
    own_counts, other_counts, assigned, lengths,
    g_hbm,
    wu0, wu1, wd0, wd1, v0, v1,
    stat_hbm, gated_hbm, slope_hbm, x1_hbm, x2_hbm,
    *rest,
):
    if not first_pass:
        rest = rest[4:]
    (
    res_hbm, gd_keep, gd_send, gu_keep, gu_send, vec_hbm,
    g_out, wu, wd, vec, stat, gated, slope, x1, x2, res, down, normed, gd, gu, acc, sums, sums_up,
    in_sem, w_sem, out_sem, gd_sem, gu_sem,
    ) = rest
    layer = 1 if first_pass else 0
    s = facts(layer, own_counts, other_counts, assigned, lengths)
    most = g_out.shape[0] // ROWS
    width = g_out.shape[1]
    units = wu.shape[1]
    chunks = units // UNITS
    blocks = s[BLOCKS]

    def load(what, block):
        target, source = (
            (g_out, g_hbm.at[s[SLOT]] if first_pass else g_hbm),
            (stat, stat_hbm), (gated, gated_hbm), (slope, slope_hbm), (x1, x1_hbm), (x2, x2_hbm),
        )[what]
        return pltpu.make_async_copy(
            source.at[rows_at(block)], target.at[rows_at(block)], in_sem.at[what, block]
        )

    @pl.when(blocks > 0)
    def _():
        fetch_start(s, vec, v0, v1, w_sem.at[0])

    for block in range(most):
        @pl.when(block < blocks)
        def _(block=block):
            for what in (0, 1, 5, 3, 4):
                load(what, block).start()

        if block == 0:
            @pl.when(blocks > 0)
            def _():
                fetch_start(s, wd, wd0, wd1, w_sem.at[2])
                fetch_start(s, wu, wu0, wu1, w_sem.at[1])

    for block in range(most):
        pl.when(block < blocks)(lambda block=block: load(2, block).start())

    sums[...] = jnp.zeros(sums.shape, F32)
    sums_up[...] = jnp.zeros(sums_up.shape, F32)

    @pl.when(blocks > 0)
    def _():
        pltpu.make_async_copy(v0, vec, w_sem.at[0]).wait()

        def step(block, carry):
            rows = rows_at(block)
            for what in (0, 1, 5):
                load(what, block).wait()
            inverse_one = stat[rows, HEADS : HEADS + 1]
            inverse_two = stat[rows, HEADS + 1 : HEADS + 2]
            gn = jnp.where(live_column(s, block), g_out[rows, :].astype(F32), 0.0)
            hat = x2[rows, :].astype(F32)
            sums[2:3, :] += jnp.sum(gn * hat, axis=0, keepdims=True)
            sums[3:4, :] += jnp.sum(gn, axis=0, keepdims=True)
            gh = gn * vec_row(vec, V_G2)
            mean_one = jnp.mean(gh, axis=-1, keepdims=True)
            mean_two = jnp.mean(gh * hat, axis=-1, keepdims=True)
            g_res = (gh - mean_one - hat * mean_two) * inverse_two
            down_b = g_res.astype(BF16)
            sums[4:5, :] += jnp.sum(down_b.astype(F32), axis=0, keepdims=True)
            down[rows, :] = down_b
            acc[...] = g_res

            @pl.when(block == 0)
            def _():
                pltpu.make_async_copy(wd0, wd, w_sem.at[2]).wait()
                pltpu.make_async_copy(wu0, wu, w_sem.at[1]).wait()

            load(3, block).wait()
            load(4, block).wait()

            def units(start, stop):
                def gate(c):
                    return dot_nt(down[rows, :], wd[c * UNITS : (c + 1) * UNITS, :])

                more = None
                later = gate(start)
                for c in range(start, stop):
                    cols = slice(c * UNITS, (c + 1) * UNITS)
                    g_gated = later
                    if c + 1 < stop:
                        later = gate(c + 1)
                    lift = (g_gated * slope[rows, cols].astype(F32)).astype(BF16)
                    slope[rows, cols] = lift
                    sums_up[0:1, cols] += jnp.sum(lift.astype(F32), axis=0, keepdims=True)
                    part = dot_nt(lift, wu[:, cols])
                    more = part if more is None else more + part
                acc[...] += more

            by_chunks(s[CHUNKS], chunks, units)
            g_normed = acc[...]
            hat = x1[rows, :].astype(F32)
            normed[rows, :] = (hat * vec_row(vec, V_G1) + vec_row(vec, V_B1)).astype(BF16)
            sums[0:1, :] += jnp.sum(g_normed * hat, axis=0, keepdims=True)
            sums[1:2, :] += jnp.sum(g_normed, axis=0, keepdims=True)
            gh = g_normed * vec_row(vec, V_G1)
            mean_one = jnp.mean(gh, axis=-1, keepdims=True)
            mean_two = jnp.mean(gh * hat, axis=-1, keepdims=True)
            res[rows, :] = (gh - mean_one - hat * mean_two) * inverse_one
            pltpu.make_async_copy(res.at[rows], res_hbm.at[rows], out_sem.at[block]).start()
            return carry

        lax.fori_loop(0, blocks, step, 0)
        for block in range(most):
            pl.when(block < blocks)(lambda block=block: load(2, block).wait())


    half_rows = units // 2
    half_cols = units // 2
    per_half = chunks // 2

    def chunk_copies(c):
        half, inside = c // per_half, c % per_half
        down_part = gd.at[cols_at(c * UNITS, UNITS), :]
        up_part = gu.at[:, cols_at(c * UNITS, UNITS)]
        place = cols_at(inside * UNITS, UNITS)
        return half, down_part, up_part, place

    def send_chunk(c):
        half, down_part, up_part, place = chunk_copies(c)

        @pl.when(half == s[SECTION])
        def _():
            pltpu.make_async_copy(down_part, gd_keep.at[layer, place, :], gd_sem.at[c]).start()
            pltpu.make_async_copy(up_part, gu_keep.at[layer, :, place], gu_sem.at[c]).start()

        @pl.when(half != s[SECTION])
        def _():
            pltpu.make_async_copy(down_part, gd_send.at[layer, place, :], gd_sem.at[c]).start()
            pltpu.make_async_copy(up_part, gu_send.at[layer, :, place], gu_sem.at[c]).start()

    def weigh(count):
        span = count * ROWS

        def one(c, carry):
            cols = cols_at(c * UNITS, UNITS)
            gd[cols, :] = dot_tn(gated[0:span, cols], down[0:span, :]).astype(BF16)
            gu[:, cols] = dot_tn(normed[0:span, :], slope[0:span, cols]).astype(BF16)
            send_chunk(c)
            return carry

        lax.fori_loop(0, s[CHUNKS], one, 0)

    clear_odd(blocks, gated, down, normed, slope)
    by_blocks(blocks, most, weigh)

    def nothing(c, carry):
        cols = cols_at(c * UNITS, UNITS)
        gd[cols, :] = jnp.zeros((UNITS, width), BF16)
        gu[:, cols] = jnp.zeros((width, UNITS), BF16)
        send_chunk(c)
        return carry

    lax.fori_loop(s[CHUNKS], chunks, nothing, 0)

    for c in range(chunks):
        _, down_part, up_part, place = chunk_copies(c)
        pltpu.make_async_copy(down_part, gd_keep.at[layer, place, :], gd_sem.at[c]).wait()
        pltpu.make_async_copy(up_part, gu_keep.at[layer, :, place], gu_sem.at[c]).wait()
    for piece in range(units // width):
        sums[8 + piece : 9 + piece, :] = sums_up[0:1, piece * width : (piece + 1) * width]
    pltpu.sync_copy(sums, vec_hbm)
    for block in range(most):
        @pl.when(block < blocks)
        def _(block=block):
            rows = rows_at(block)
            pltpu.make_async_copy(res.at[rows], res_hbm.at[rows], out_sem.at[block]).wait()


def ffn_back(first_pass, scalars, g_out, weights, saved, grads=()):
    length, width = g_out.shape[-2:]
    units = weights[4].shape[1]
    blocks = length // ROWS
    chunks = units // UNITS
    shape = jax.ShapeDtypeStruct
    _, _, stat, gated, slope, x1, x2 = saved
    return pl.pallas_call(
        functools.partial(ffn_back_kernel, first_pass),
        out_shape=[
            shape((length, width), F32),
            shape((2, units // 2, width), BF16),
            shape((2, units // 2, width), BF16),
            shape((2, width, units // 2), BF16),
            shape((2, width, units // 2), BF16),
            shape((16, width), F32),
        ],
        in_specs=[SMEM] * 4 + [HBM] * (12 + len(grads)),
        out_specs=[HBM] * 6,
        input_output_aliases={16 + i: 1 + i for i in range(len(grads))},
        scratch_shapes=[
            pltpu.VMEM((length, width), BF16),
            pltpu.VMEM((width, units), BF16),
            pltpu.VMEM((units, width), BF16),
            pltpu.VMEM(weights[8].shape, BF16),
            pltpu.VMEM((length, 128), F32),
            pltpu.VMEM((length, units), BF16),
            pltpu.VMEM((length, units), BF16),
            pltpu.VMEM((length, width), BF16),
            pltpu.VMEM((length, width), BF16),
            pltpu.VMEM((length, width), F32),
            pltpu.VMEM((length, width), BF16),
            pltpu.VMEM((length, width), BF16),
            pltpu.VMEM((units, width), BF16),
            pltpu.VMEM((width, units), BF16),
            pltpu.VMEM((ROWS, width), F32),
            pltpu.VMEM((16, width), F32),
            pltpu.VMEM((8, units), F32),
            pltpu.SemaphoreType.DMA((6, blocks)),
            pltpu.SemaphoreType.DMA((3,)),
            pltpu.SemaphoreType.DMA((blocks,)),
            pltpu.SemaphoreType.DMA((chunks,)),
            pltpu.SemaphoreType.DMA((chunks,)),
        ],
        compiler_params=pltpu.CompilerParams(vmem_limit_bytes=VMEM_BYTES),
        name="ffn_back",
    )(*scalars, g_out, *weights[4:8], *weights[8:10], stat, gated, slope, x1, x2, *grads)


def attention_back_kernel(
    first_layer,
    own_counts, other_counts, assigned, lengths,
    res_hbm, g_hbm, x_hbm,
    wq0, wq1, wo0, wo1,
    proj_hbm, ctx_hbm, stat_hbm, ffn_sums_hbm,
    *rest,
):
    layer = 0 if first_layer else 1
    s = facts(layer, own_counts, other_counts, assigned, lengths)
    rest = rest[3 if first_layer else 0 :]
    if first_layer:
        in_keep, in_send = rest[:2]
        rest = rest[2:]
    else:
        in_hbm = rest[0]
        rest = rest[1:]
    (
        ga_keep, ga_send,
        res, g_in, h, wq, wo, proj, ctx, stat, attn, g_ctx, g_proj, rows_log, rows_delta,
        go, gq, out_a, out_b, sums, ffn_sums, extra,
        in_sem, w_sem, out_sem, go_sem, gq_sem, extra_sem,
    ) = rest
    most = res.shape[0] // ROWS
    width = res.shape[1]
    half = width // 2
    pairs_all = width // 128
    blocks = s[BLOCKS]
    live = s[LIVE]
    lane = lax.broadcasted_iota(jnp.int32, (1, 128), 1)
    low = lane < 64
    zero_pair = jnp.zeros((1, 128), BF16)

    def load(what, block):
        target, source = (
            (res, res_hbm), (ctx, ctx_hbm), (stat, stat_hbm), (proj, proj_hbm),
            (h, x_hbm.at[s[SLOT]] if first_layer else x_hbm),
        )[what]
        return pltpu.make_async_copy(
            source.at[rows_at(block)], target.at[rows_at(block)], in_sem.at[what, block]
        )

    def load_g(block):
        source = g_hbm if first_layer else g_hbm.at[s[SLOT]]
        return pltpu.make_async_copy(
            source.at[rows_at(block)], g_in.at[rows_at(block)], in_sem.at[0, block]
        )

    for what in (0, 1):
        for block in range(most):
            pl.when(block < blocks)(lambda what=what, block=block: load(what, block).start())

    @pl.when(blocks > 0)
    def _():
        fetch_start(s, wo, wo0, wo1, w_sem.at[0])

    for what in (2, 3, 4):
        for block in range(most):
            pl.when(block < blocks)(lambda what=what, block=block: load(what, block).start())

    @pl.when(blocks > 0)
    def _():
        fetch_start(s, wq, wq0, wq1, w_sem.at[1])

    sums[...] = jnp.zeros(sums.shape, F32)
    ffn_load = pltpu.make_async_copy(ffn_sums_hbm, ffn_sums, extra_sem.at[2])
    ffn_load.start()

    def out_copies(block, wait):
        rows = rows_at(block)
        if first_layer:
            copies = [
                pltpu.make_async_copy(out_a.at[rows], in_keep.at[rows], out_sem.at[0, block]),
                pltpu.make_async_copy(out_b.at[rows], in_send.at[1, rows], out_sem.at[1, block]),
            ]
        else:
            copies = [pltpu.make_async_copy(out_b.at[rows], in_hbm.at[rows], out_sem.at[0, block])]
        for copy in copies:
            copy.wait() if wait else copy.start()

    def emit(block, value):
        rows = rows_at(block)
        if first_layer:
            front = s[SECTION] == 0
            out_a[rows, :] = jnp.where(front, value[:, :half], value[:, half:])
            out_b[rows, :] = jnp.where(front, value[:, half:], value[:, :half]).astype(BF16)
        else:
            out_b[rows, :] = value.astype(BF16)
        out_copies(block, False)

    def go_copy(part, keep):
        target = (ga_keep if keep else ga_send).at[layer, 0:width, 0:half]
        return pltpu.make_async_copy(go.at[:, part * half : (part + 1) * half], target, go_sem.at[part])

    def gq_copy(part, keep):
        target = (ga_keep if keep else ga_send).at[layer, 0:width, half : 4 * half]
        cols = slice(part * 3 * half, (part + 1) * 3 * half)
        return pltpu.make_async_copy(gq.at[:, cols], target, gq_sem.at[part])

    def start_halves(make):
        for part in range(2):
            pl.when(s[SECTION] == part)(lambda part=part: make(part, True).start())
            pl.when(s[SECTION] != part)(lambda part=part: make(part, False).start())

    @pl.when(blocks > 0)
    def _():
        pltpu.make_async_copy(wo0, wo, w_sem.at[0]).wait()
        spread = spread_heads(width)

        def before(block, carry):
            rows = rows_at(block)
            load(0, block).wait()
            load(1, block).wait()
            attn_b = res[rows, :].astype(BF16)
            attn[rows, :] = attn_b
            sums[2:3, :] += jnp.sum(attn_b.astype(F32), axis=0, keepdims=True)
            g_context = dot_nt(attn_b, wo[...]).astype(BF16)
            g_ctx[rows, :] = g_context
            product = (g_context.astype(F32) * ctx[rows, :].astype(F32)).astype(BF16)
            rows_delta[:, rows] = dot_nt(spread, product)
            load(2, block).wait()
            rows_log[:, rows] = stat[rows, :].T
            load(3, block).wait()
            return carry

        lax.fori_loop(0, blocks, before, 0)
        clear_odd(blocks, proj, g_ctx, ctx, attn, h)

        @pl.when(blocks % 2 == 1)
        def _():
            rows_log[:, rows_at(blocks)] = jnp.zeros((128, ROWS), F32)
            rows_delta[:, rows_at(blocks)] = jnp.zeros((128, ROWS), F32)

        def weigh_out(count):
            span = count * ROWS
            go[...] = dot_tn(ctx[0:span, :], attn[0:span, :]).astype(BF16)

        by_blocks(blocks, most, weigh_out)
        start_halves(go_copy)

        for pair in range(pairs_all):
            @pl.when(pair >= s[PAIRS])
            def _(pair=pair):
                for part in range(3):
                    cols = slice(part * width + pair * 128, part * width + (pair + 1) * 128)
                    g_proj[:, cols] = jnp.zeros((g_proj.shape[0], 128), BF16)

        def attend_back(count):
            span = count * ROWS

            def one_pair(pair, carry):
                cols = cols_at(pair * 128, 128)
                total_q = None
                for block in range(count):
                    rows = rows_at(block)
                    q = proj[0:span, cols]
                    d_ctx = g_ctx[0:span, cols]
                    k = proj[rows, cols_at(width + pair * 128, 128)] * jnp.asarray(0.125, BF16)
                    v = proj[rows, cols_at(2 * width + pair * 128, 128)]
                    fill = jnp.where(live_column(s, block), 0.0, NEG_FILL) if block >= count - 2 else 0.0
                    found_k, found_v, found_q = [], [], []
                    for head, own in ((0, low), (1, ~low)):
                        k_own = jnp.where(own, k, zero_pair)
                        v_own = jnp.where(own, v, zero_pair)
                        log_row = rows_log[pl.ds(2 * pair + head, 1), 0:span]
                        delta_row = rows_delta[pl.ds(2 * pair + head, 1), 0:span]
                        probs = jnp.exp(dot_nt(k_own, q) + fill - log_row)
                        g_probs = dot_nt(v_own, d_ctx)
                        g_scores = (probs * (g_probs - delta_row)).astype(BF16)
                        found_v.append(dot(probs.astype(BF16), d_ctx))
                        found_k.append(dot(g_scores, q))
                        found_q.append(dot_tn(g_scores, k_own))
                    more_q = found_q[0] + found_q[1]
                    total_q = more_q if block == 0 else total_q + more_q
                    g_k = jnp.where(low, found_k[0], found_k[1]) * 0.125
                    g_v = jnp.where(low, found_v[0], found_v[1])
                    g_proj[rows, cols_at(width + pair * 128, 128)] = g_k.astype(BF16)
                    g_proj[rows, cols_at(2 * width + pair * 128, 128)] = g_v.astype(BF16)
                g_proj[0:span, cols] = total_q.astype(BF16)
                return carry

            lax.fori_loop(0, s[PAIRS], one_pair, 0)

        by_blocks(blocks, most, attend_back)

        for block in range(most):
            pl.when(block < blocks)(lambda block=block: load(4, block).wait())
        pltpu.make_async_copy(wq0, wq, w_sem.at[1]).wait()

        def weigh_in(count):
            span = count * ROWS

            def one(part, carry):
                cols = cols_at(part * width, width)
                gq[:, cols] = dot_tn(h[0:span, :], g_proj[0:span, cols]).astype(BF16)
                return carry

            lax.fori_loop(0, 3, one, 0)

        by_blocks(blocks, most, weigh_in)
        start_halves(gq_copy)

        def after(block, carry):
            rows = rows_at(block)
            grad = g_proj[rows, :]
            sums[0:1, :] += jnp.sum(grad[:, :width].astype(F32), axis=0, keepdims=True)
            sums[1:2, :] += jnp.sum(grad[:, 2 * width :].astype(F32), axis=0, keepdims=True)
            emit(block, res[rows, :] + dot_nt(grad, wq[...]))
            return carry

        lax.fori_loop(0, blocks, after, 0)

    @pl.when(s[SKIP] == 1)
    def _():
        go[...] = jnp.zeros(go.shape, BF16)
        gq[...] = jnp.zeros(gq.shape, BF16)
        start_halves(go_copy)
        start_halves(gq_copy)
        for block in range(most):
            pl.when(block < live)(lambda block=block: load_g(block).start())
        for block in range(most):
            pl.when(block < live)(lambda block=block: load_g(block).wait())

        def carry_on(block, carry):
            value = g_in[rows_at(block), :].astype(F32)
            emit(block, jnp.where(live_column(s, block), value, 0.0))
            return carry

        lax.fori_loop(0, live, carry_on, 0)

    if first_layer:
        def clear(block, carry):
            emit(block, jnp.zeros((ROWS, width), F32))
            return carry

        lax.fori_loop(live, most, clear, 0)

    ffn_load.wait()
    own_sums = jnp.concatenate([sums[...], jnp.zeros(sums.shape, F32)], axis=0)
    extra[...] = jnp.concatenate([ffn_sums[...], own_sums], axis=1).astype(BF16)
    extra_copies = [
        pltpu.make_async_copy(extra, target.at[layer, width : width + 16], extra_sem.at[at])
        for at, target in enumerate((ga_keep, ga_send))
    ]
    for copy in extra_copies:
        copy.start()
    for copy in extra_copies:
        copy.wait()
    for part in range(2):
        go_copy(part, True).wait()
        gq_copy(part, True).wait()
    for block in range(most):
        if first_layer:
            out_copies(block, True)
        else:
            pl.when(block < live)(lambda block=block: out_copies(block, True))


def attention_back(first_layer, scalars, res, g_out, x, weights, saved, ffn_sums, grads=()):
    length, width = res.shape
    blocks = length // ROWS
    shape = jax.ShapeDtypeStruct
    proj, ctx, stat = saved[:3]
    outs = (
        [shape((length, width // 2), F32), shape((2, length, width // 2), BF16)]
        if first_layer
        else [shape((length, width), BF16)]
    )
    outs += [
        shape((2, width + 16, 2 * width), BF16),
        shape((2, width + 16, 2 * width), BF16),
    ]
    return pl.pallas_call(
        functools.partial(attention_back_kernel, first_layer),
        out_shape=outs,
        in_specs=[SMEM] * 4 + [HBM] * (11 + len(grads)),
        out_specs=[HBM] * len(outs),
        input_output_aliases={15 + i: len(outs) - len(grads) + i for i in range(len(grads))},
        scratch_shapes=[
            pltpu.VMEM((length, width), F32),
            pltpu.VMEM((length, width), BF16),
            pltpu.VMEM((length, width), BF16),
            pltpu.VMEM((width, 3 * width), BF16),
            pltpu.VMEM((width, width), BF16),
            pltpu.VMEM((length, 3 * width), BF16),
            pltpu.VMEM((length, width), BF16),
            pltpu.VMEM((length, 128), F32),
            pltpu.VMEM((length, width), BF16),
            pltpu.VMEM((length, width), BF16),
            pltpu.VMEM((length, 3 * width), BF16),
            pltpu.VMEM((128, length), F32),
            pltpu.VMEM((128, length), F32),
            pltpu.VMEM((width, width), BF16),
            pltpu.VMEM((width, 3 * width), BF16),
            pltpu.VMEM((length if first_layer else 8, width // 2), F32),
            pltpu.VMEM((length, width // 2 if first_layer else width), BF16),
            pltpu.VMEM((8, width), F32),
            pltpu.VMEM((16, width), F32),
            pltpu.VMEM((16, 2 * width), BF16),
            pltpu.SemaphoreType.DMA((5, blocks)),
            pltpu.SemaphoreType.DMA((2,)),
            pltpu.SemaphoreType.DMA((2, blocks)),
            pltpu.SemaphoreType.DMA((2,)),
            pltpu.SemaphoreType.DMA((2,)),
            pltpu.SemaphoreType.DMA((3,)),
        ],
        compiler_params=pltpu.CompilerParams(vmem_limit_bytes=VMEM_BYTES),
        name="attention_back",
    )(*scalars, res, g_out, x, *weights[0:4], proj, ctx, stat, ffn_sums, *grads)


def swap(part):
    return lax.ppermute(part, "section", [(0, 1), (1, 0)])


def across(part, bit):
    pairs = [(i, i ^ 1 << bit) for i in range(lax.axis_size("dp"))]
    return lax.ppermute(part, "dp", pairs)


FREE = pl.CostEstimate(flops=0, bytes_accessed=0, transcendentals=0)
SHORT = pl.CostEstimate(flops=4_000_000_000, bytes_accessed=0, transcendentals=0)
LONG = pl.CostEstimate(flops=20_000_000_000, bytes_accessed=0, transcendentals=0)


def my_bit(bit):
    return (lax.axis_index("dp") >> bit) & 1


def half_sum_kernel(bit, turn, extra, keep, got, before, out, own, new, in_sem, out_sem):
    layers, rows, _ = keep.shape
    half = (rows - extra) // 2
    at = 1 - my_bit(bit) if turn == 0 else my_bit(bit)
    spans = [(pl.ds(pl.multiple_of(at * half, 16), half), slice(0, half))]
    if extra:
        spans.append((slice(rows - extra, rows), slice(half, half + extra)))

    def loads(layer):
        copies = []
        for i, (source, target) in enumerate(spans):
            for j, (ref, held) in enumerate(((keep, own), (got, new))):
                copies.append(
                    pltpu.make_async_copy(
                        ref.at[layer, source], held.at[layer, target], in_sem.at[layer, i, j]
                    )
                )
        return copies

    def store(layer):
        return pltpu.make_async_copy(own.at[layer], out.at[layer], out_sem.at[layer])

    for layer in range(layers):
        for copy in loads(layer):
            copy.start()
    for layer in range(layers):
        for copy in loads(layer):
            copy.wait()

        def add_rows(i, carry, layer=layer):
            place = pl.ds(pl.multiple_of(i * 16, 16), 16)
            total = own[layer, place, :].astype(F32) + new[layer, place, :].astype(F32)
            own[layer, place, :] = total.astype(BF16)
            return carry

        lax.fori_loop(0, (half + extra) // 16, add_rows, 0, unroll=3)
        store(layer).start()
    for layer in range(layers):
        store(layer).wait()


def half_sum(bit, turn, extra, keep, got, before):
    layers, rows, cols = keep.shape
    half = (rows - extra) // 2
    if half % 48:
        at = 1 - my_bit(bit) if turn == 0 else my_bit(bit)

        def parts(a):
            own = lax.dynamic_slice_in_dim(a, at * half, half, 1)
            return jnp.concatenate([own, a[:, rows - extra :]], axis=1).astype(F32)

        return (parts(keep) + parts(got)).astype(BF16)
    return pl.pallas_call(
        functools.partial(half_sum_kernel, bit, turn, extra),
        out_shape=jax.ShapeDtypeStruct((layers, half + extra, cols), BF16),
        in_specs=[HBM, HBM, HBM],
        out_specs=HBM,
        scratch_shapes=[
            pltpu.VMEM((layers, half + extra, cols), BF16),
            pltpu.VMEM((layers, half + extra, cols), BF16),
            pltpu.SemaphoreType.DMA((layers, 2, 2)),
            pltpu.SemaphoreType.DMA((layers,)),
        ],
        compiler_params=pltpu.CompilerParams(vmem_limit_bytes=VMEM_BYTES),
        cost_estimate=FREE if turn else SHORT,
        name="half_sum",
    )(keep, got, before)


def split_kernel(extra, one, two, before, own, send, *vec):
    layers, rows, _ = one.shape
    rows -= extra
    section = lax.axis_index("section")
    mine, theirs = (section, 1 - section) if layers == 2 else (0, 0)

    def total(at, where):
        return (one[pl.ds(at, 1), where].astype(F32) + two[pl.ds(at, 1), where].astype(F32)).astype(BF16)

    own[...] = total(mine, slice(0, rows))
    send[...] = total(theirs, slice(0, rows))
    if extra:
        vec[0][...] = total(mine, slice(rows, rows + extra))


def split(one, two, before, extra):
    layers, rows, cols = one.shape
    rows -= extra
    if rows % 16:
        total = (one.astype(F32) + two.astype(F32)).astype(BF16)
        own = send = total
        if layers == 2:
            section = lax.axis_index("section")
            own = lax.dynamic_slice_in_dim(total, section, 1)
            send = lax.dynamic_slice_in_dim(total, 1 - section, 1)
        return (own[:, :rows], send[:, :rows]) + ((own[:, rows:],) if extra else ())
    whole = pl.BlockSpec(memory_space=pltpu.VMEM)
    outs = [jax.ShapeDtypeStruct((1, rows, cols), BF16)] * 2
    if extra:
        outs.append(jax.ShapeDtypeStruct((1, extra, cols), BF16))
    return pl.pallas_call(
        functools.partial(split_kernel, extra),
        out_shape=outs,
        in_specs=[whole, whole, HBM],
        out_specs=[whole] * len(outs),
        cost_estimate=SHORT,
        name="split",
    )(one, two, before)


def join_kernel(bit, part, got, before, both, held, in_sem, out_sem):
    layers, rows, _ = part.shape
    mine = my_bit(bit)
    steps = [(at, layer) for at in range(2) for layer in range(layers)]

    def load(at, layer):
        source = (part, got)[at].at[layer]
        return pltpu.make_async_copy(source, held.at[at, layer], in_sem.at[at, layer])

    def store(at, layer):
        place = mine if at == 0 else 1 - mine
        target = both.at[layer, pl.ds(pl.multiple_of(place * rows, 16), rows)]
        return pltpu.make_async_copy(held.at[at, layer], target, out_sem.at[at, layer])

    for step in steps:
        load(*step).start()
    for step in steps:
        load(*step).wait()
        store(*step).start()
    for step in steps:
        store(*step).wait()


def join(bit, part, got, before):
    layers, rows, cols = part.shape
    if rows % 16:
        at = jnp.arange(2)[:, None, None]
        both = jnp.where(at == my_bit(bit), part[:, None], got[:, None])
        return both.reshape(layers, 2 * rows, cols)
    return pl.pallas_call(
        functools.partial(join_kernel, bit),
        out_shape=jax.ShapeDtypeStruct((layers, 2 * rows, cols), BF16),
        in_specs=[HBM, HBM, HBM],
        out_specs=HBM,
        scratch_shapes=[
            pltpu.VMEM((2, layers, rows, cols), BF16),
            pltpu.SemaphoreType.DMA((2, layers)),
            pltpu.SemaphoreType.DMA((2, layers)),
        ],
        compiler_params=pltpu.CompilerParams(vmem_limit_bytes=VMEM_BYTES),
        cost_estimate=SHORT,
        name="join",
    )(part, got, before)


class Stream:
    def __init__(self, layers, keep, send, order, extra):
        self.layers, self.keep, self.send, self.order, self.extra = layers, keep, send, order, extra

    def enter(self):
        self.got = swap(self.send)

    def send_half(self, turn, chain):
        bit = self.order[turn]
        self.old = (self.keep, self.got)
        send = half_sum(bit, 0, self.extra, *self.old, chain[-1])
        chain.append(send)
        self.got = across(send, bit)

    def keep_half(self, turn, chain):
        self.keep = half_sum(self.order[turn], 1, self.extra, *self.old, chain[-1])
        chain.append(self.keep)

    def exchange(self, chain):
        self.own, send, *self.vec = split(self.keep, self.got, chain[-1], self.extra)
        chain.append(send)
        if len(self.layers) == 1:
            live = self.layers[0]
            self.got = lax.ppermute(send, "section", [(1 - live, live)])
        else:
            self.got = swap(send)

    def gather(self, turn, chain):
        bits = len(self.order)
        bit = self.order[bits - 1 - turn]
        if turn == 0:
            place = jnp.arange(2)[:, None, None]
            self.part = jnp.where(place == lax.axis_index("section"), self.own, self.got)
        else:
            self.part = join(self.order[bits - turn], self.part, self.got, chain[-1])
        chain.append(self.part)
        if len(self.layers) == 1:
            devices = lax.axis_size("dp")
            first = self.layers[0] * devices
            pairs = [(first + i, first + (i ^ 1 << bit)) for i in range(devices)]
            self.got = lax.ppermute(self.part, ("section", "dp"), pairs)
        else:
            self.got = across(self.part, bit)


def place_kernel(kind, turn, layers, first_bit, part, *refs):
    outs_count = 2 if kind == "attn" else 1
    refs = refs[outs_count + 1 if turn else 1 :]
    outs = refs[:outs_count]
    held, wide, in_sem, out_sem = refs[outs_count:]
    rows, cols = held.shape[1:]
    side = my_bit(first_bit) if turn == 0 else 1 - my_bit(first_bit)
    live = True if len(layers) == 2 else lax.axis_index("section") == layers[0]

    def target(half, at):
        if kind == "rows":
            return outs[0].at[0, pl.ds(pl.multiple_of((2 * half + side) * rows, 8), rows), :]
        at_rows = pl.ds(pl.multiple_of(side * rows, 8), rows)
        width = cols if kind == "cols" else (cols // 4 if at == 0 else 3 * cols // 4)
        return outs[at].at[0, at_rows, half * width : (half + 1) * width]

    def out_copies(half, wait):
        pieces = [(0, slice(0, cols))]
        if kind == "attn":
            pieces = [(0, slice(0, cols // 4)), (1, slice(cols // 4, cols))]
        for at, where in pieces:
            copy = pltpu.make_async_copy(wide.at[half, :, where], target(half, at), out_sem.at[half, at])
            copy.wait() if wait else copy.start()

    def load(half):
        return pltpu.make_async_copy(part.at[half], held.at[half], in_sem.at[half])

    for half in range(2):
        load(half).start()
    for half in range(2):
        load(half).wait()

        def convert(i, carry, half=half):
            at = pl.ds(pl.multiple_of(i * 16, 16), 16)
            value = held[half, at, :].astype(F32)
            wide[half, at, :] = value if live is True else jnp.where(live, value, 0.0)
            return carry

        lax.fori_loop(0, rows // 16, convert, 0, unroll=2)
        out_copies(half, False)
    for half in range(2):
        out_copies(half, True)


def place(kind, turn, layers, first_bit, part, shapes, extra):
    rows, cols = part.shape[1:]
    return pl.pallas_call(
        functools.partial(place_kernel, kind, turn, layers, first_bit),
        out_shape=[jax.ShapeDtypeStruct(out, F32) for out in shapes],
        in_specs=[HBM] * (1 + len(extra)),
        out_specs=[HBM] * len(shapes),
        input_output_aliases={1 + i: i for i in range(len(shapes))} if turn else {},
        scratch_shapes=[
            pltpu.VMEM((2, rows, cols), BF16),
            pltpu.VMEM((2, rows, cols), F32),
            pltpu.SemaphoreType.DMA((2,)),
            pltpu.SemaphoreType.DMA((2, 2)),
        ],
        compiler_params=pltpu.CompilerParams(vmem_limit_bytes=VMEM_BYTES),
        cost_estimate=LONG,
        name="place_" + kind,
    )(part, *extra)


def slots_kernel(index, keep, got, before, out, own, new, wide, in_sem, out_sem):
    section = lax.axis_index("section")
    mine = pltpu.make_async_copy(keep, own, in_sem.at[0])
    theirs = pltpu.make_async_copy(got.at[index], new, in_sem.at[1])
    mine.start()
    theirs.start()
    mine.wait()
    store_mine = pltpu.make_async_copy(own, out.at[section], out_sem.at[0])
    store_mine.start()
    theirs.wait()

    def convert(i, carry):
        at = pl.ds(pl.multiple_of(i * 32, 32), 32)
        wide[at, :] = new[at, :].astype(F32)
        return carry

    lax.fori_loop(0, new.shape[0] // 32, convert, 0)
    store_theirs = pltpu.make_async_copy(wide, out.at[1 - section], out_sem.at[1])
    store_theirs.start()
    store_mine.wait()
    store_theirs.wait()


def both_slots(index, keep, got, before):
    return pl.pallas_call(
        functools.partial(slots_kernel, index),
        out_shape=jax.ShapeDtypeStruct((2, *keep.shape), F32),
        in_specs=[HBM, HBM, HBM],
        out_specs=HBM,
        scratch_shapes=[
            pltpu.VMEM(keep.shape, F32),
            pltpu.VMEM(keep.shape, BF16),
            pltpu.VMEM(keep.shape, F32),
            pltpu.SemaphoreType.DMA((2,)),
            pltpu.SemaphoreType.DMA((2,)),
        ],
        compiler_params=pltpu.CompilerParams(vmem_limit_bytes=VMEM_BYTES),
        cost_estimate=FREE,
        name="both_slots",
    )(keep, got, before)


def tail(layers, grads, out_keep, in_keep, sends, weight_shapes):
    bits = lax.axis_size("dp").bit_length() - 1
    by_x = list(range(bits))
    orders = (by_x[:1] + by_x[2:] + by_x[1:2], [1, 0] + by_x[2:], by_x[2:-1] + [1, 0] + by_x[-1:])
    streams = []
    for (keep, send), order in zip(grads, orders):
        extra = keep.shape[1] - keep.shape[2] // 2 if keep is grads[2][0] else 0
        if len(layers) == 1:
            keep, send = [a[layers[0] : layers[0] + 1] for a in (keep, send)]
        streams.append(Stream(layers, keep, send, order, extra))
    for stream in streams:
        stream.enter()
    slots_got = swap(sends)
    chain = [sends]
    for turn in range(bits):
        for stream in streams:
            stream.send_half(turn, chain)
        for stream in streams:
            stream.keep_half(turn, chain)
        if turn == 0:
            out_half = both_slots(0, out_keep, slots_got, chain[-1])
            grad_half = both_slots(1, in_keep, slots_got, out_half)
            chain.append(grad_half)
    for stream in streams:
        stream.exchange(chain)
    for turn in range(bits):
        for stream in streams:
            stream.gather(turn, chain)
    kinds = ("rows", "cols", "attn")
    placed, results = [], []
    for kind, stream, shapes in zip(kinds, streams, weight_shapes):
        placed.append(place(kind, 0, layers, stream.order[0], stream.part, shapes, [chain[-1]]))
        chain.append(placed[-1][0])
    for kind, stream, shapes, half in zip(kinds, streams, weight_shapes, placed):
        half = [*half, chain[-1]]
        results += place(kind, 1, layers, stream.order[0], stream.got, shapes, half)
        chain.append(results[-1])
    vec = streams[2].vec[0][0].astype(F32)
    if len(layers) == 1:
        vec = jnp.where(lax.axis_index("section") == layers[0], vec, 0.0)
    return (*results, vec, out_half, grad_half)


def on_device(
    inputs, cotangent, lengths, assignment, skip_flags, head_counts, ffn_counts,
    w_qkv, bias_q, bias_v, w_out, bias_out, norm1_gain, norm1_bias, w_up, bias_up, w_down,
    bias_down, norm2_gain, norm2_bias,
):
    section = lax.axis_index("section")
    first = section == 0
    slots, length, width = inputs.shape
    units = w_up.shape[2]
    zeros = jnp.zeros((1, width), BF16)
    own_counts = jnp.concatenate([skip_flags, head_counts, ffn_counts], axis=0).reshape(3 * MICRO)
    coded = jnp.concatenate([own_counts // 64, own_counts % 64]).astype(BF16).reshape(1, 6 * MICRO)
    own_vec = jnp.concatenate(
        [
            bias_q, zeros, bias_v, bias_out, norm1_gain, norm1_bias,
            bias_up.reshape(units // width, width),
            bias_down, norm2_gain, norm2_bias,
            jnp.pad(coded, ((0, 0), (0, width - 6 * MICRO))), zeros, zeros,
        ],
        axis=0,
    )
    other_vec = swap(own_vec)
    codes = other_vec[13, : 6 * MICRO].astype(jnp.int32)
    other_counts = codes[: 3 * MICRO] * 64 + codes[3 * MICRO :]
    weights = []
    for mine in (w_qkv[0], w_out[0], w_up[0], w_down[0]):
        weights += [mine, swap(mine)]
    weights += [own_vec, other_vec]
    scalars = [own_counts, other_counts, assignment, lengths]

    early = weights[:2] * 4 + weights[8:]
    proj, ctx, stat = layer_forward(False, "attend", scalars, inputs, early)
    passed, *saved_one = layer_forward(
        False, "finish", scalars, inputs, weights[2:4] + weights[2:], [ctx, stat]
    )
    saved_one = [proj, ctx, *saved_one]
    out_keep, sends, *saved_two = layer_forward(True, "all", scalars, passed, weights)
    saved_two = saved_two[:2] + saved_two[3:]

    res, *ffn, sums = ffn_back(True, scalars, cotangent, weights, saved_two)
    g_mid, *attn = attention_back(
        False, scalars, res, cotangent, passed, weights, saved_two, sums
    )
    res, *ffn, sums = ffn_back(False, scalars, g_mid, weights, saved_one, ffn)
    in_keep, sends, *attn = attention_back(
        True, scalars, res, g_mid, inputs, weights, saved_one, sums, [sends, *attn]
    )

    grads = (ffn[:2], ffn[2:], attn)
    weight_shapes = (
        [(1, units, width)], [(1, width, units)], [(1, width, width), (1, width, 3 * width)],
    )
    skips = [jnp.where(section == layer, own_counts, other_counts)[:MICRO] for layer in range(2)]
    used = [jnp.sum(skip) < MICRO for skip in skips]
    which = jnp.where(used[0] & used[1], 0, jnp.where(used[0], 1, 2))
    branches = [
        functools.partial(tail, layers, weight_shapes=weight_shapes) for layers in ((0, 1), (0,), (1,))
    ]
    grad_w_down, grad_w_up, grad_w_out, grad_w_qkv, vec, out_half, grad_half = lax.switch(
        which, branches, grads, out_keep, in_keep, sends
    )
    by_ffn, by_attn = vec[:, :width], vec[:, width:]
    grad_bias_up = by_ffn[8 : 8 + units // width].reshape(1, units)
    return (
        out_half, grad_half, grad_w_qkv, by_attn[0:1], by_attn[1:2], grad_w_out, by_attn[2:3],
        by_ffn[0:1], by_ffn[1:2], grad_w_up, grad_bias_up, grad_w_down, by_ffn[4:5], by_ffn[2:3],
        by_ffn[3:4],
    )


def solution(mesh):
    three, two = P("section", None, None), P("section", None)
    return jax.shard_map(
        on_device,
        mesh=mesh,
        in_specs=(
            P("dp", None, None), P("dp", None, None), P(), P("dp"),
            P(None, "section"), P(None, "section"), P(None, "section"),
            three, two, two, three, two, two, two, three, two, three, two, two, two,
        ),
        out_specs=(
            P("dp", None, "section"), P("dp", None, "section"),
            three, two, two, three, two, two, two, three, two, three, two, two, two,
        ),
        check_vma=False,
    )
```

profile of v0, /device:TPU:0, one launch (start us, length us, event | category | flops | bytes accessed | tf_op | source)
XLA Modules:
  0.0 650.1 jit_solution(781803289122861844)
XLA Ops:
  10.4 22.4 %layer_forward_attend.1 = (bf16[1024,2304]{1,0:T(8,128)(2,1)}, bf16[1024,768]{1,0:T(8,128)(2,1)}, f32[1024,128]{1,0:T(8,128)}) custom-call(s32[6]{0:T(128)} %copy-done.18, s32[6]{0:T(128)} %copy-done.19, s32[2]{0:T(128)} %assigned.13, s32[32]{0:T(128)} %lengths.13, bf16[2,1024,768]{2,1,0:T(8,128)(2,1)} %x_hbm.5, bf16[768,2304]{1,0:T(8,128)(2,1)} %bitcast.70, ...), custom_call_target="tpu_custom_call" | custom-call | flops 60000002048 | tf_op jit(solution)/shard_map/layer_forward_attend/pallas_call | solution.py:482
  32.8 19.0 %layer_forward_finish.1 = (bf16[1024,768]{1,0:T(8,128)(2,1)}, f32[1024,128]{1,0:T(8,128)}, bf16[1024,3072]{1,0:T(8,128)(2,1)}, bf16[1024,3072]{1,0:T(8,128)(2,1)...) custom-call(s32[6]{0:T(128)} %copy-done.18, s32[6]{0:T(128)} %copy-done.19, s32[2]{0:T(128)} %assigned.13, ...), custom_call_target="tpu_custom_call" | custom-call | flops 10000000000 | tf_op jit(solution)/shard_map/layer_forward_finish/pallas_call | solution.py:482
  55.5 11.8 %ffn_back.2 = (f32[1024,768]{1,0:T(8,128)}, bf16[2,1536,768]{2,1,0:T(8,128)(2,1)}, bf16[2,1536,768]{2,1,0:T(8,128)(2,1)}, bf16[2,768,1536]{2,1,0:T(8,128)(2,1)},...) custom-call(s32[6]{0:T(128)} %copy-done.18, s32[6]{0:T(128)} %copy-done.19, s32[2]{0:T(128)} %assigned.13, s32[32]{0:T(128)} %lengths.13, ...), custom_call_target="tpu_custom_call" | custom-call | tf_op jit(solution)/shard_map/ffn_back/pallas_call | solution.py:711
  67.3 12.7 %attention_back.2 = (bf16[1024,768]{1,0:T(8,128)(2,1)}, bf16[2,784,1536]{2,1,0:T(8,128)(2,1)}, bf16[2,784,1536]{2,1,0:T(8,128)(2,1)}) custom-call(s32[6]{0:T(128)} %copy-done.18, s32[6]{0:T(128)} %copy-done.19, s32[2]{0:T(128)} %assigned.13, s32[32]{0:T(128)} %lengths.13, f32[1024,768]{1,0:T(8,128)} %get-tuple-element.199.res_hbm, ...), custom_call_target="tpu_custom_call" | custom-call | tf_op jit(solution)/shard_map/attention_back/pallas_call | solution.py:1025
  80.0 23.4 %ffn_back.3 = (f32[1024,768]{1,0:T(8,128)}, bf16[2,1536,768]{2,1,0:T(8,128)(2,1)}, bf16[2,1536,768]{2,1,0:T(8,128)(2,1)}, bf16[2,768,1536]{2,1,0:T(8,128)(2,1)},...) custom-call(s32[6]{0:T(128)} %copy-done.18, ...), custom_call_target="tpu_custom_call", output_to_operand_aliasing={{1}: (16, {}), {2}: (17, {}), {3}: (18, {}), {4}: (19, {})} | custom-call | tf_op jit(solution)/shard_map/ffn_back/pallas_call | solution.py:711
  103.5 24.9 %attention_back.3 = (f32[1024,384]{1,0:T(8,128)}, bf16[2,1024,384]{2,1,0:T(8,128)(2,1)}, bf16[2,784,1536]{2,1,0:T(8,128)(2,1)}, bf16[2,784,1536]{2,1,0:T(8,128)(2,1)}) custom-call(s32[6]{0:T(128)} %copy-done.18, s32[6]{0:T(128)} %copy-done.19, s32[2]{0:T(128)} %assigned.13, ...), custom_call_target="tpu_custom_call", output_to_operand_aliasing={{1}: (15, {}), {2}: (16, {}), {3}: (17, {})} | custom-call | tf_op jit(solution)/shard_map/attention_back/pallas_call | solution.py:1025
  128.4 520.6 %conditional.1 = (f32[1,3072,768]{2,1,0:T(8,128)}, f32[1,768,3072]{2,1,0:T(8,128)}, f32[1,768,768]{2,1,0:T(8,128)}, f32[1,768,2304]{2,1,0:T(8,128)}, f32[16,1536...) conditional(s32[]{:T(128)} %clamp.3, ...), branch_computations={%region_2.3_spmd, %region_3.4_spmd, %region_4.5_spmd} | conditional | flops 216000446464 | bytes 217032192 | solution.py:1488
  128.4 43.0 %collective-permute-start = (bf16[2,1536,768]{2,1,0:T(8,128)(2,1)}, bf16[2,1536,768]{2,1,0:T(8,128)(2,1)}, u32[]{:S(2)}, u32[]{:S(2)}) collective-permute-start(bf16[2,1536,768]{2,1,0:T(8,128)(2,1)} %get-tuple-element.65), channel_id=1, source_target_pairs={{0,16},{16,0},{1,17},{17,1},{2,18},{18,2},{3,19},{19,3},{4,20},{20... | collective-permute-start | bytes 14155784 | tf_op jit(solution)/shard_map/cond/branch_0_fun/ppermute | solution.py:1065
  171.9 7.4 %collective-permute-done.got = bf16[2,1536,768]{2,1,0:T(8,128)(2,1)} collective-permute-done((bf16[2,1536,768]{2,1,0:T(8,128)(2,1)}, bf16[2,1536,768]{2,1,0:T(8,128)(2,1)}, u32[]{:S(2)}, u32[]{:S(2)}) %collective-permute-start) | collective-permute-done | bytes 4718624 | tf_op jit(solution)/shard_map/cond/branch_0_fun/ppermute | solution.py:1065
  179.3 3.8 half_sum.72.before
  183.1 129.2 %collective-permute-start.3 = (bf16[2,768,768]{2,1,0:T(8,128)(2,1)}, bf16[2,768,768]{2,1,0:T(8,128)(2,1)}, u32[]{:S(2)}, u32[]{:S(2)}) collective-permute-start(bf16[2,768,768]{2,1,0:T(8,128)(2,1)} %half_sum.72.before), channel_id=1, source_target_pairs={{0,1},{1,0},{2,3},{3,2},{4,5},{5,4},{6,7},{7,6},{8,9},{9,8},{10,11... | collective-permute-start | bytes 7077896 | tf_op jit(solution)/shard_map/cond/branch_0_fun/ppermute | solution.py:1070
  312.3 3.8 half_sum.73.before
  316.1 10.8 %collective-permute-start.5 = (bf16[2,384,1536]{2,1,0:T(8,128)(2,1)}, bf16[2,384,1536]{2,1,0:T(8,128)(2,1)}, u32[]{:S(2)}, u32[]{:S(2)}) collective-permute-start(bf16[2,384,1536]{2,1,0:T(8,128)(2,1)} %half_sum.73.before), channel_id=1, source_target_pairs={{0,2},{1,3},{2,0},{3,1},{4,6},{5,7},{6,4},{7,5},{8,10},{9,11},{10,... | collective-permute-start | bytes 7077896 | tf_op jit(solution)/shard_map/cond/branch_0_fun/ppermute | solution.py:1070
  326.8 3.8 half_sum.74.before
  330.7 4.5 collective-permute-start.4
  335.3 3.8 half_sum.75.before.keep
  339.1 3.8 half_sum.76.before.keep
  342.9 3.8 half_sum.77.before.keep
  353.0 11.4 %collective-permute-done.3.got = bf16[2,768,768]{2,1,0:T(8,128)(2,1)} collective-permute-done((bf16[2,768,768]{2,1,0:T(8,128)(2,1)}, bf16[2,768,768]{2,1,0:T(8,128)(2,1)}, u32[]{:S(2)}, u32[]{:S(2)}) %collective-permute-start.3) | collective-permute-done | bytes 2359328 | tf_op jit(solution)/shard_map/cond/branch_0_fun/ppermute | solution.py:1070
  367.1 11.0 %collective-permute-start.7 = (bf16[2,384,768]{2,1,0:T(8,128)(2,1)}, bf16[2,384,768]{2,1,0:T(8,128)(2,1)}, u32[]{:S(2)}, u32[]{:S(2)}) collective-permute-start(bf16[2,384,768]{2,1,0:T(8,128)(2,1)} %half_sum.78.before), channel_id=1, source_target_pairs={{0,4},{1,5},{2,6},{3,7},{4,0},{5,1},{6,2},{7,3},{8,12},{9,13},{10,... | collective-permute-start | bytes 3538952 | tf_op jit(solution)/shard_map/cond/branch_0_fun/ppermute | solution.py:1070
  384.5 5.2 collective-permute-done.4.got
  402.7 12.0 %collective-permute-done.7.got = bf16[2,384,768]{2,1,0:T(8,128)(2,1)} collective-permute-done((bf16[2,384,768]{2,1,0:T(8,128)(2,1)}, bf16[2,384,768]{2,1,0:T(8,128)(2,1)}, u32[]{:S(2)}, u32[]{:S(2)}) %collective-permute-start.7) | collective-permute-done | bytes 1179680 | tf_op jit(solution)/shard_map/cond/branch_0_fun/ppermute | solution.py:1070
  432.3 13.6 %collective-permute-done.10.got = bf16[2,192,768]{2,1,0:T(8,128)(2,1)} collective-permute-done((bf16[2,192,768]{2,1,0:T(8,128)(2,1)}, bf16[2,192,768]{2,1,0:T(8,128)(2,1)}, u32[]{:S(2)}, u32[]{:S(2)}) %collective-permute-start.10) | collective-permute-done | bytes 589856 | tf_op jit(solution)/shard_map/cond/branch_0_fun/ppermute | solution.py:1070
  464.0 11.7 %collective-permute-done.17.two = bf16[2,48,1536]{2,1,0:T(8,128)(2,1)} collective-permute-done((bf16[2,48,1536]{2,1,0:T(8,128)(2,1)}, bf16[2,48,1536]{2,1,0:T(8,128)(2,1)}, u32[]{:S(2)}, u32[]{:S(2)}) %collective-permute-start.17) | collective-permute-done | bytes 294944 | tf_op jit(solution)/shard_map/cond/branch_0_fun/ppermute | solution.py:1070
  479.4 3.9 collective-permute-done.16.two
  494.0 29.6 %collective-permute-done.22.got = bf16[2,48,1536]{2,1,0:T(8,128)(2,1)} collective-permute-done((bf16[2,48,1536]{2,1,0:T(8,128)(2,1)}, bf16[2,48,1536]{2,1,0:T(8,128)(2,1)}, u32[]{:S(2)}, u32[]{:S(2)}) %collective-permute-start.22) | collective-permute-done | bytes 294944 | tf_op jit(solution)/shard_map/cond/branch_0_fun/ppermute | solution.py:1070
  525.6 4.5 collective-permute-done.20.got
  533.3 9.3 %collective-permute-done.19.got = bf16[2,192,768]{2,1,0:T(8,128)(2,1)} collective-permute-done((bf16[2,192,768]{2,1,0:T(8,128)(2,1)}, bf16[2,192,768]{2,1,0:T(8,128)(2,1)}, u32[]{:S(2)}, u32[]{:S(2)}) %collective-permute-start.19) | collective-permute-done | bytes 589856 | tf_op jit(solution)/shard_map/cond/branch_0_fun/ppermute | solution.py:1070
  544.8 10.5 %collective-permute-done.25.got = bf16[2,96,1536]{2,1,0:T(8,128)(2,1)} collective-permute-done((bf16[2,96,1536]{2,1,0:T(8,128)(2,1)}, bf16[2,96,1536]{2,1,0:T(8,128)(2,1)}, u32[]{:S(2)}, u32[]{:S(2)}) %collective-permute-start.25) | collective-permute-done | bytes 589856 | tf_op jit(solution)/shard_map/cond/branch_0_fun/ppermute | solution.py:1070
  565.2 15.3 %collective-permute-done.23.got = bf16[2,384,768]{2,1,0:T(8,128)(2,1)} collective-permute-done((bf16[2,384,768]{2,1,0:T(8,128)(2,1)}, bf16[2,384,768]{2,1,0:T(8,128)(2,1)}, u32[]{:S(2)}, u32[]{:S(2)}) %collective-permute-start.23) | collective-permute-done | bytes 1179680 | tf_op jit(solution)/shard_map/cond/branch_0_fun/ppermute | solution.py:1070
  591.8 3.8 place_rows.6.refs_0_
  603.0 33.6 %collective-permute-done.26.part = bf16[2,768,768]{2,1,0:T(8,128)(2,1)} collective-permute-done((bf16[2,768,768]{2,1,0:T(8,128)(2,1)}, bf16[2,768,768]{2,1,0:T(8,128)(2,1)}, u32[]{:S(2)}, u32[]{:S(2)}) %collective-permute-start.26) | collective-permute-done | bytes 2359328 | tf_op jit(solution)/shard_map/cond/branch_0_fun/ppermute | solution.py:1070
  (131 shorter events, 138.3 us)
Async XLA Ops:
  5.1 27.7 %collective-permute-start.96 = (bf16[768,768]{1,0:T(8,128)(2,1)}, bf16[768,768]{1,0:T(8,128)(2,1)}, u32[]{:S(2)}, u32[]{:S(2)}) collective-permute-start(bf16[768,768]{1,0:T(8,128)(2,1)} %bitcast.77), channel_id=1, source_target_pairs={{0,16},{16,0},{1,17},{17,1},{2,18},{18,2},{3,19},{19,3},{4,20},{20... | collective-permute-start | bytes 3538952 | tf_op jit(solution)/shard_map/ppermute | solution.py:1065
  5.6 27.2 %collective-permute-start.94 = (bf16[768,3072]{1,0:T(8,128)(2,1)}, bf16[768,3072]{1,0:T(8,128)(2,1)}, u32[]{:S(2)}, u32[]{:S(2)}) collective-permute-start(bf16[768,3072]{1,0:T(8,128)(2,1)} %bitcast.59), channel_id=1, source_target_pairs={{0,16},{16,0},{1,17},{17,1},{2,18},{18,2},{3,19},{19,3},{4,20},{20... | collective-permute-start | bytes 14155784 | tf_op jit(solution)/shard_map/ppermute | solution.py:1065
  5.6 27.2 %collective-permute-start.95 = (bf16[3072,768]{1,0:T(8,128)(2,1)}, bf16[3072,768]{1,0:T(8,128)(2,1)}, u32[]{:S(2)}, u32[]{:S(2)}) collective-permute-start(bf16[3072,768]{1,0:T(8,128)(2,1)} %bitcast.64), channel_id=1, source_target_pairs={{0,16},{16,0},{1,17},{17,1},{2,18},{18,2},{3,19},{19,3},{4,20},{20... | collective-permute-start | bytes 14155784 | tf_op jit(solution)/shard_map/ppermute | solution.py:1065
  128.4 50.9 %collective-permute-start = (bf16[2,1536,768]{2,1,0:T(8,128)(2,1)}, bf16[2,1536,768]{2,1,0:T(8,128)(2,1)}, u32[]{:S(2)}, u32[]{:S(2)}) collective-permute-start(bf16[2,1536,768]{2,1,0:T(8,128)(2,1)} %get-tuple-element.65), channel_id=1, source_target_pairs={{0,16},{16,0},{1,17},{17,1},{2,18},{18,2},{3,19},{19,3},{4,20},{20... | collective-permute-start | bytes 14155784 | tf_op jit(solution)/shard_map/cond/branch_0_fun/ppermute | solution.py:1065
  171.4 140.9 %collective-permute-start.2 = (bf16[2,768,1536]{2,1,0:T(8,128)(2,1)}, bf16[2,768,1536]{2,1,0:T(8,128)(2,1)}, u32[]{:S(2)}, u32[]{:S(2)}) collective-permute-start(bf16[2,768,1536]{2,1,0:T(8,128)(2,1)} %get-tuple-element.69), channel_id=1, source_target_pairs={{0,16},{16,0},{1,17},{17,1},{2,18},{18,2},{3,19},{19,3},{4,20},{20... | collective-permute-start | bytes 14155784 | tf_op jit(solution)/shard_map/cond/branch_0_fun/ppermute | solution.py:1065
  171.5 155.3 %collective-permute-start.1 = (bf16[2,784,1536]{2,1,0:T(8,128)(2,1)}, bf16[2,784,1536]{2,1,0:T(8,128)(2,1)}, u32[]{:S(2)}, u32[]{:S(2)}) collective-permute-start(bf16[2,784,1536]{2,1,0:T(8,128)(2,1)} %get-tuple-element.67), channel_id=1, source_target_pairs={{0,16},{16,0},{1,17},{17,1},{2,18},{18,2},{3,19},{19,3},{4,20},{20... | collective-permute-start | bytes 14450696 | tf_op jit(solution)/shard_map/cond/branch_0_fun/ppermute | solution.py:1065
  183.1 181.2 %collective-permute-start.3 = (bf16[2,768,768]{2,1,0:T(8,128)(2,1)}, bf16[2,768,768]{2,1,0:T(8,128)(2,1)}, u32[]{:S(2)}, u32[]{:S(2)}) collective-permute-start(bf16[2,768,768]{2,1,0:T(8,128)(2,1)} %half_sum.72.before), channel_id=1, source_target_pairs={{0,1},{1,0},{2,3},{3,2},{4,5},{5,4},{6,7},{7,6},{8,9},{9,8},{10,11... | collective-permute-start | bytes 7077896 | tf_op jit(solution)/shard_map/cond/branch_0_fun/ppermute | solution.py:1070
  316.1 62.6 %collective-permute-start.5 = (bf16[2,384,1536]{2,1,0:T(8,128)(2,1)}, bf16[2,384,1536]{2,1,0:T(8,128)(2,1)}, u32[]{:S(2)}, u32[]{:S(2)}) collective-permute-start(bf16[2,384,1536]{2,1,0:T(8,128)(2,1)} %half_sum.73.before), channel_id=1, source_target_pairs={{0,2},{1,3},{2,0},{3,1},{4,6},{5,7},{6,4},{7,5},{8,10},{9,11},{10,... | collective-permute-start | bytes 7077896 | tf_op jit(solution)/shard_map/cond/branch_0_fun/ppermute | solution.py:1070
  330.7 59.0 %collective-permute-start.4 = (bf16[2,400,1536]{2,1,0:T(8,128)(2,1)}, bf16[2,400,1536]{2,1,0:T(8,128)(2,1)}, u32[]{:S(2)}, u32[]{:S(2)}) collective-permute-start(bf16[2,400,1536]{2,1,0:T(8,128)(2,1)} %half_sum.74.before), channel_id=1, source_target_pairs={{0,4},{1,5},{2,6},{3,7},{4,0},{5,1},{6,2},{7,3},{8,12},{9,13},{10,... | collective-permute-start | bytes 7372808 | tf_op jit(solution)/shard_map/cond/branch_0_fun/ppermute | solution.py:1070
  335.2 11.6 %collective-permute-start.6 = (bf16[2,1024,384]{2,1,0:T(8,128)(2,1)}, bf16[2,1024,384]{2,1,0:T(8,128)(2,1)}, u32[]{:S(2)}, u32[]{:S(2)}) collective-permute-start(bf16[2,1024,384]{2,1,0:T(8,128)(2,1)} %get-tuple-element.70.before), channel_id=1, source_target_pairs={{0,16},{16,0},{1,17},{17,1},{2,18},{18,2},{3,19},{19,3},{4,20},{20... | collective-permute-start | bytes 4718600 | tf_op jit(solution)/shard_map/cond/branch_0_fun/ppermute | solution.py:1065
  367.1 47.6 %collective-permute-start.7 = (bf16[2,384,768]{2,1,0:T(8,128)(2,1)}, bf16[2,384,768]{2,1,0:T(8,128)(2,1)}, u32[]{:S(2)}, u32[]{:S(2)}) collective-permute-start(bf16[2,384,768]{2,1,0:T(8,128)(2,1)} %half_sum.78.before), channel_id=1, source_target_pairs={{0,4},{1,5},{2,6},{3,7},{4,0},{5,1},{6,2},{7,3},{8,12},{9,13},{10,... | collective-permute-start | bytes 3538952 | tf_op jit(solution)/shard_map/cond/branch_0_fun/ppermute | solution.py:1070
  381.3 38.1 %collective-permute-start.9 = (bf16[2,192,1536]{2,1,0:T(8,128)(2,1)}, bf16[2,192,1536]{2,1,0:T(8,128)(2,1)}, u32[]{:S(2)}, u32[]{:S(2)}) collective-permute-start(bf16[2,192,1536]{2,1,0:T(8,128)(2,1)} %half_sum.79.before), channel_id=1, source_target_pairs={{0,1},{1,0},{2,3},{3,2},{4,5},{5,4},{6,7},{7,6},{8,9},{9,8},{10,11... | collective-permute-start | bytes 3538952 | tf_op jit(solution)/shard_map/cond/branch_0_fun/ppermute | solution.py:1070
  392.4 30.9 %collective-permute-start.8 = (bf16[2,208,1536]{2,1,0:T(8,128)(2,1)}, bf16[2,208,1536]{2,1,0:T(8,128)(2,1)}, u32[]{:S(2)}, u32[]{:S(2)}) collective-permute-start(bf16[2,208,1536]{2,1,0:T(8,128)(2,1)} %half_sum.80.before), channel_id=1, source_target_pairs={{0,2},{1,3},{2,0},{3,1},{4,6},{5,7},{6,4},{7,5},{8,10},{9,11},{10,... | collective-permute-start | bytes 3833864 | tf_op jit(solution)/shard_map/cond/branch_0_fun/ppermute | solution.py:1070
  416.8 29.1 %collective-permute-start.10 = (bf16[2,192,768]{2,1,0:T(8,128)(2,1)}, bf16[2,192,768]{2,1,0:T(8,128)(2,1)}, u32[]{:S(2)}, u32[]{:S(2)}) collective-permute-start(bf16[2,192,768]{2,1,0:T(8,128)(2,1)} %half_sum.84.before), channel_id=1, source_target_pairs={{0,8},{1,9},{2,10},{3,11},{4,12},{5,13},{6,14},{7,15},{8,0},{9,1},... | collective-permute-start | bytes 1769480 | tf_op jit(solution)/shard_map/cond/branch_0_fun/ppermute | solution.py:1070
  421.6 27.8 %collective-permute-start.12 = (bf16[2,96,1536]{2,1,0:T(8,128)(2,1)}, bf16[2,96,1536]{2,1,0:T(8,128)(2,1)}, u32[]{:S(2)}, u32[]{:S(2)}) collective-permute-start(bf16[2,96,1536]{2,1,0:T(8,128)(2,1)} %half_sum.85.before), channel_id=1, source_target_pairs={{0,4},{1,5},{2,6},{3,7},{4,0},{5,1},{6,2},{7,3},{8,12},{9,13},{10,... | collective-permute-start | bytes 1769480 | tf_op jit(solution)/shard_map/cond/branch_0_fun/ppermute | solution.py:1070
  425.5 25.8 %collective-permute-start.11 = (bf16[2,112,1536]{2,1,0:T(8,128)(2,1)}, bf16[2,112,1536]{2,1,0:T(8,128)(2,1)}, u32[]{:S(2)}, u32[]{:S(2)}) collective-permute-start(bf16[2,112,1536]{2,1,0:T(8,128)(2,1)} %half_sum.86.before), channel_id=1, source_target_pairs={{0,1},{1,0},{2,3},{3,2},{4,5},{5,4},{6,7},{7,6},{8,9},{9,8},{10,11... | collective-permute-start | bytes 2064392 | tf_op jit(solution)/shard_map/cond/branch_0_fun/ppermute | solution.py:1070
  447.8 14.4 %collective-permute-start.13 = (bf16[2,96,768]{2,1,0:T(8,128)(2,1)}, bf16[2,96,768]{2,1,0:T(8,128)(2,1)}, u32[]{:S(2)}, u32[]{:S(2)}) collective-permute-start(bf16[2,96,768]{2,1,0:T(8,128)(2,1)} %half_sum.90.before), channel_id=1, source_target_pairs={{0,2},{1,3},{2,0},{3,1},{4,6},{5,7},{6,4},{7,5},{8,10},{9,11},{10,... | collective-permute-start | bytes 884744 | tf_op jit(solution)/shard_map/cond/branch_0_fun/ppermute | solution.py:1070
  451.3 24.4 %collective-permute-start.17 = (bf16[2,48,1536]{2,1,0:T(8,128)(2,1)}, bf16[2,48,1536]{2,1,0:T(8,128)(2,1)}, u32[]{:S(2)}, u32[]{:S(2)}) collective-permute-start(bf16[2,48,1536]{2,1,0:T(8,128)(2,1)} %half_sum.91.before), channel_id=1, source_target_pairs={{0,8},{1,9},{2,10},{3,11},{4,12},{5,13},{6,14},{7,15},{8,0},{9,1},... | collective-permute-start | bytes 884744 | tf_op jit(solution)/shard_map/cond/branch_0_fun/ppermute | solution.py:1070
  453.4 30.0 %collective-permute-start.16 = (bf16[2,64,1536]{2,1,0:T(8,128)(2,1)}, bf16[2,64,1536]{2,1,0:T(8,128)(2,1)}, u32[]{:S(2)}, u32[]{:S(2)}) collective-permute-start(bf16[2,64,1536]{2,1,0:T(8,128)(2,1)} %half_sum.92.before), channel_id=1, source_target_pairs={{0,8},{1,9},{2,10},{3,11},{4,12},{5,13},{6,14},{7,15},{8,0},{9,1},... | collective-permute-start | bytes 1179656 | tf_op jit(solution)/shard_map/cond/branch_0_fun/ppermute | solution.py:1070
  464.0 13.5 %collective-permute-start.14 = (bf16[1,96,768]{2,1,0:T(8,128)(2,1)}, bf16[1,96,768]{2,1,0:T(8,128)(2,1)S(1)}, u32[]{:S(2)}, u32[]{:S(2)}) collective-permute-start(bf16[1,96,768]{2,1,0:T(8,128)(2,1)} %get-tuple-element.74.before), channel_id=1, source_target_pairs={{0,16},{16,0},{1,17},{17,1},{2,18},{18,2},{3,19},{19,3},{4,20},{20... | collective-permute-start | bytes 442376 | tf_op jit(solution)/shard_map/cond/branch_0_fun/ppermute | solution.py:1065
  477.6 14.4 %collective-permute-start.15 = (bf16[2,96,768]{2,1,0:T(8,128)(2,1)S(1)}, bf16[2,96,768]{2,1,0:T(8,128)(2,1)}, u32[]{:S(2)}, u32[]{:S(2)}) collective-permute-start(bf16[2,96,768]{2,1,0:T(8,128)(2,1)S(1)} %broadcast_select_fusion.2.part), channel_id=1, source_target_pairs={{0,2},{1,3},{2,0},{3,1},{4,6},{5,7},{6,4},{7,5},{8,10},{9,11},{10,... | collective-permute-start | bytes 884744 | tf_op jit(solution)/shard_map/cond/branch_0_fun/ppermute | solution.py:1070
  489.1 34.5 %collective-permute-start.22 = (bf16[2,48,1536]{2,1,0:T(8,128)(2,1)}, bf16[2,48,1536]{2,1,0:T(8,128)(2,1)}, u32[]{:S(2)}, u32[]{:S(2)}) collective-permute-start(bf16[2,48,1536]{2,1,0:T(8,128)(2,1)} %get-tuple-element.255.part), channel_id=1, source_target_pairs={{0,8},{1,9},{2,10},{3,11},{4,12},{5,13},{6,14},{7,15},{8,0},{9,1},... | collective-permute-start | bytes 884744 | tf_op jit(solution)/shard_map/cond/branch_0_fun/ppermute | solution.py:1070
  489.1 40.9 %collective-permute-start.20 = (bf16[2,48,1536]{2,1,0:T(8,128)(2,1)}, bf16[2,48,1536]{2,1,0:T(8,128)(2,1)}, u32[]{:S(2)}, u32[]{:S(2)}) collective-permute-start(bf16[2,48,1536]{2,1,0:T(8,128)(2,1)} %get-tuple-element.256.before.part), channel_id=1, source_target_pairs={{0,8},{1,9},{2,10},{3,11},{4,12},{5,13},{6,14},{7,15},{8,0},{9,1},... | collective-permute-start | bytes 884744 | tf_op jit(solution)/shard_map/cond/branch_0_fun/ppermute | solution.py:1070
  493.9 48.7 %collective-permute-start.19 = (bf16[2,192,768]{2,1,0:T(8,128)(2,1)}, bf16[2,192,768]{2,1,0:T(8,128)(2,1)}, u32[]{:S(2)}, u32[]{:S(2)}) collective-permute-start(bf16[2,192,768]{2,1,0:T(8,128)(2,1)} %join.27.before.part), channel_id=1, source_target_pairs={{0,8},{1,9},{2,10},{3,11},{4,12},{5,13},{6,14},{7,15},{8,0},{9,1},... | collective-permute-start | bytes 1769480 | tf_op jit(solution)/shard_map/cond/branch_0_fun/ppermute | solution.py:1070
  525.5 29.8 %collective-permute-start.25 = (bf16[2,96,1536]{2,1,0:T(8,128)(2,1)}, bf16[2,96,1536]{2,1,0:T(8,128)(2,1)}, u32[]{:S(2)}, u32[]{:S(2)}) collective-permute-start(bf16[2,96,1536]{2,1,0:T(8,128)(2,1)} %join.28.before.part), channel_id=1, source_target_pairs={{0,4},{1,5},{2,6},{3,7},{4,0},{5,1},{6,2},{7,3},{8,12},{9,13},{10,... | collective-permute-start | bytes 1769480 | tf_op jit(solution)/shard_map/cond/branch_0_fun/ppermute | solution.py:1070
  531.9 26.8 %collective-permute-start.24 = (bf16[2,96,1536]{2,1,0:T(8,128)(2,1)}, bf16[2,96,1536]{2,1,0:T(8,128)(2,1)}, u32[]{:S(2)}, u32[]{:S(2)}) collective-permute-start(bf16[2,96,1536]{2,1,0:T(8,128)(2,1)} %join.29.before.part), channel_id=1, source_target_pairs={{0,1},{1,0},{2,3},{3,2},{4,5},{5,4},{6,7},{7,6},{8,9},{9,8},{10,11... | collective-permute-start | bytes 1769480 | tf_op jit(solution)/shard_map/cond/branch_0_fun/ppermute | solution.py:1070
  544.7 35.8 %collective-permute-start.23 = (bf16[2,384,768]{2,1,0:T(8,128)(2,1)}, bf16[2,384,768]{2,1,0:T(8,128)(2,1)}, u32[]{:S(2)}, u32[]{:S(2)}) collective-permute-start(bf16[2,384,768]{2,1,0:T(8,128)(2,1)} %join.30.before.part), channel_id=1, source_target_pairs={{0,4},{1,5},{2,6},{3,7},{4,0},{5,1},{6,2},{7,3},{8,12},{9,13},{10,... | collective-permute-start | bytes 3538952 | tf_op jit(solution)/shard_map/cond/branch_0_fun/ppermute | solution.py:1070
  557.3 28.2 %collective-permute-start.28 = (bf16[2,192,1536]{2,1,0:T(8,128)(2,1)}, bf16[2,192,1536]{2,1,0:T(8,128)(2,1)}, u32[]{:S(2)}, u32[]{:S(2)}) collective-permute-start(bf16[2,192,1536]{2,1,0:T(8,128)(2,1)} %join.31.before.part), channel_id=1, source_target_pairs={{0,1},{1,0},{2,3},{3,2},{4,5},{5,4},{6,7},{7,6},{8,9},{9,8},{10,11... | collective-permute-start | bytes 3538952 | tf_op jit(solution)/shard_map/cond/branch_0_fun/ppermute | solution.py:1070
  560.8 28.4 %collective-permute-start.27 = (bf16[2,192,1536]{2,1,0:T(8,128)(2,1)}, bf16[2,192,1536]{2,1,0:T(8,128)(2,1)}, u32[]{:S(2)}, u32[]{:S(2)}) collective-permute-start(bf16[2,192,1536]{2,1,0:T(8,128)(2,1)} %join.32.before.part), channel_id=1, source_target_pairs={{0,2},{1,3},{2,0},{3,1},{4,6},{5,7},{6,4},{7,5},{8,10},{9,11},{10,... | collective-permute-start | bytes 3538952 | tf_op jit(solution)/shard_map/cond/branch_0_fun/ppermute | solution.py:1070
  583.1 53.6 %collective-permute-start.26 = (bf16[2,768,768]{2,1,0:T(8,128)(2,1)}, bf16[2,768,768]{2,1,0:T(8,128)(2,1)}, u32[]{:S(2)}, u32[]{:S(2)}) collective-permute-start(bf16[2,768,768]{2,1,0:T(8,128)(2,1)} %join.33.before.part), channel_id=1, source_target_pairs={{0,1},{1,0},{2,3},{3,2},{4,5},{5,4},{6,7},{7,6},{8,9},{9,8},{10,11... | collective-permute-start | bytes 7077896 | tf_op jit(solution)/shard_map/cond/branch_0_fun/ppermute | solution.py:1070
  588.0 52.6 %collective-permute-start.29 = (bf16[2,384,1536]{2,1,0:T(8,128)(2,1)}, bf16[2,384,1536]{2,1,0:T(8,128)(2,1)}, u32[]{:S(2)}, u32[]{:S(2)}) collective-permute-start(bf16[2,384,1536]{2,1,0:T(8,128)(2,1)} %join.34.before.part), channel_id=1, source_target_pairs={{0,2},{1,3},{2,0},{3,1},{4,6},{5,7},{6,4},{7,5},{8,10},{9,11},{10,... | collective-permute-start | bytes 7077896 | tf_op jit(solution)/shard_map/cond/branch_0_fun/ppermute | solution.py:1070
  591.7 52.7 %collective-permute-start.30 = (bf16[2,384,1536]{2,1,0:T(8,128)(2,1)}, bf16[2,384,1536]{2,1,0:T(8,128)(2,1)}, u32[]{:S(2)}, u32[]{:S(2)}) collective-permute-start(bf16[2,384,1536]{2,1,0:T(8,128)(2,1)} %join.35.refs_0_.part), channel_id=1, source_target_pairs={{0,4},{1,5},{2,6},{3,7},{4,0},{5,1},{6,2},{7,3},{8,12},{9,13},{10,... | collective-permute-start | bytes 7077896 | tf_op jit(solution)/shard_map/cond/branch_0_fun/ppermute | solution.py:1070
  (13 other events, 77.4 us)
where the time goes:
time: 653 us; the launch traced here: 650 us
  Pallas kernels  235 us (36%)
  starting transfers between devices  227 us (35%)
  waiting for transfers between devices  171 us (26%)
  local copies, waits for them, and re-layouts  7.05 us (1%)
    ppermute x24, starting transfers between devices, across(): return lax.ppermute(part, 'dp', pairs)  181 us
    ppermute x24, waiting for transfers between devices, across(): return lax.ppermute(part, 'dp', pairs)  162 us
    pallas_call x24, Pallas kernels, half_sum(): pl.pallas_call(functools.partial(half_sum_kernel, bit, turn, extra), out_...  63.6 us
    ppermute x12, starting transfers between devices, swap(): return lax.ppermute(part, 'section', [(0, 1), (1, 0)])  45.2 us
    pallas_call x3, Pallas kernels, layer_forward(): pl.pallas_call(functools.partial(forward_kernel, last, phase), out_shape=...  45.1 us
    pallas_call x2, Pallas kernels, attention_back(): pl.pallas_call(functools.partial(attention_back_kernel, first_layer), out...  37.6 us
    pallas_call x2, Pallas kernels, ffn_back(): pl.pallas_call(functools.partial(ffn_back_kernel, first_pass), out_shape=...  35.3 us
    pallas_call x6, Pallas kernels, place(): pl.pallas_call(functools.partial(place_kernel, kind, turn, layers, first_...  22.4 us
  transfers between devices with their start and end apart: 36, of which 17 were waited for; matrix products, arithmetic and copies ran while one was open for 2% of the time, Pallas kernels for 21%

commit v1 on v0

--- a/solution.py
+++ b/solution.py
@@ -65,15 +65,16 @@
 
 
 def by_blocks(count, most, body):
-    for blocks in range(2, most + 1, 2):
-        pl.when((count == blocks) | (count == blocks - 1))(functools.partial(body, blocks))
-
-
-def clear_odd(count, *refs):
-    @pl.when(count % 2 == 1)
-    def _():
+    pl.when(count > 0)(functools.partial(body, most))
+
+
+def clear_dead(count, *refs):
+    def clear(block, carry):
         for ref in refs:
-            ref[rows_at(count), :] = jnp.zeros((ROWS, ref.shape[1]), ref.dtype)
+            ref[rows_at(block), :] = jnp.zeros((ROWS, ref.shape[1]), ref.dtype)
+        return carry
+
+    lax.fori_loop(count, refs[0].shape[0] // ROWS, clear, 0)
 
 
 def by_chunks(count, most, body):
@@ -238,7 +239,7 @@
 
         lax.fori_loop(0, blocks, project, 0)
 
-        clear_odd(blocks, proj)
+        clear_dead(blocks, proj)
         for pair in range(pairs_all):
             @pl.when(pair >= s[PAIRS])
             def _(pair=pair):
@@ -268,8 +269,7 @@
                     v = proj[keys, cols_at(2 * width + pair * 128, 128)]
                     for head, own in enumerate((low, ~low)):
                         scores = dot_nt(q_own[head], k)
-                        if part >= count - 2:
-                            scores = scores + fills[part]
+                        scores = scores + fills[part]
                         exps = jnp.exp(scores).astype(BF16)
                         more = dot(exps, jnp.where(own, v, ones))
                         found[head] = more if part == 0 else found[head] + more
@@ -675,7 +675,7 @@
 
         lax.fori_loop(0, s[CHUNKS], one, 0)
 
-    clear_odd(blocks, gated, down, normed, slope)
+    pl.when(blocks > 0)(lambda: clear_dead(blocks, gated, down, normed, slope))
     by_blocks(blocks, most, weigh)
 
     def nothing(c, carry):
@@ -876,12 +876,14 @@
             return carry
 
         lax.fori_loop(0, blocks, before, 0)
-        clear_odd(blocks, proj, g_ctx, ctx, attn, h)
-
-        @pl.when(blocks % 2 == 1)
-        def _():
-            rows_log[:, rows_at(blocks)] = jnp.zeros((128, ROWS), F32)
-            rows_delta[:, rows_at(blocks)] = jnp.zeros((128, ROWS), F32)
+        clear_dead(blocks, proj, g_ctx, ctx, attn, h)
+
+        def clear_columns(block, carry):
+            rows_log[:, rows_at(block)] = jnp.zeros((128, ROWS), F32)
+            rows_delta[:, rows_at(block)] = jnp.zeros((128, ROWS), F32)
+            return carry
+
+        lax.fori_loop(blocks, most, clear_columns, 0)
 
         def weigh_out(count):
             span = count * ROWS
@@ -909,7 +911,7 @@
                     d_ctx = g_ctx[0:span, cols]
                     k = proj[rows, cols_at(width + pair * 128, 128)] * jnp.asarray(0.125, BF16)
                     v = proj[rows, cols_at(2 * width + pair * 128, 128)]
-                    fill = jnp.where(live_column(s, block), 0.0, NEG_FILL) if block >= count - 2 else 0.0
+                    fill = jnp.where(live_column(s, block), 0.0, NEG_FILL)
                     found_k, found_v, found_q = [], [], []
                     for head, own in ((0, low), (1, ~low)):
                         k_own = jnp.where(own, k, zero_pair)

time: 653 us -> 563 us (0.86); the launches traced: 650 us -> 552 us
  starting transfers between devices: 227 us -> 71.8 us
  Pallas kernels: 235 us -> 267 us
  loops' own time: 1.33 us -> 15.1 us
  waiting for transfers between devices: 171 us -> 183 us
    ppermute x24, starting transfers between devices: 181 us -> 69.6 us  [across(): return lax.ppermute(part, 'dp', pairs)]
    ppermute x12, starting transfers between devices: 45.2 us -> 2.21 us  [swap(): return lax.ppermute(part, 'section', [(0, 1), (1, 0)])]
    pallas_call x2, Pallas kernels: 37.6 us -> 53 us  [attention_back(): pl.pallas_call(functools.partial(attention_back_kernel, first_layer), out...]
    another operation x1, loops' own time: 1.33 us -> 15.1 us  [on_device(): lax.switch(which, branches, grads, out_keep, in_keep, sends)]
    ppermute x12, waiting for transfers between devices: 8.38 us -> 21.3 us  [swap(): return lax.ppermute(part, 'section', [(0, 1), (1, 0)])]
    pallas_call x2, Pallas kernels: 35.3 us -> 48 us  [ffn_back(): pl.pallas_call(functools.partial(ffn_back_kernel, first_pass), out_shape=...]
  transfers between devices with their start and end apart: 36 -> 36, of which waited for: 17 -> 20; matrix products, arithmetic and copies ran while one was open for 2% -> 2% of each run, Pallas kernels for 21% -> 21%
where the time goes in v1:
time: 563 us; the launch traced here: 552 us
  Pallas kernels  267 us (47%)
  waiting for transfers between devices  183 us (33%)
  starting transfers between devices  71.8 us (13%)
  loops' own time  15.1 us (3%)
  local copies, waits for them, and re-layouts  7.05 us (1%)
  other arithmetic  6.23 us (1%)
    ppermute x24, waiting for transfers between devices, across(): return lax.ppermute(part, 'dp', pairs)  162 us
    ppermute x24, starting transfers between devices, across(): return lax.ppermute(part, 'dp', pairs)  69.6 us
    pallas_call x24, Pallas kernels, half_sum(): pl.pallas_call(functools.partial(half_sum_kernel, bit, turn, extra), out_...  63.6 us
    pallas_call x2, Pallas kernels, attention_back(): pl.pallas_call(functools.partial(attention_back_kernel, first_layer), out...  53 us
    pallas_call x3, Pallas kernels, layer_forward(): pl.pallas_call(functools.partial(forward_kernel, last, phase), out_shape=...  48.9 us
    pallas_call x2, Pallas kernels, ffn_back(): pl.pallas_call(functools.partial(ffn_back_kernel, first_pass), out_shape=...  48 us
    pallas_call x6, Pallas kernels, place(): pl.pallas_call(functools.partial(place_kernel, kind, turn, layers, first_...  22.4 us
    ppermute x12, waiting for transfers between devices, swap(): return lax.ppermute(part, 'section', [(0, 1), (1, 0)])  21.3 us
  transfers between devices with their start and end apart: 36, of which 20 were waited for; matrix products, arithmetic and copies ran while one was open for 2% of the time, Pallas kernels for 21%

profile of v1, /device:TPU:0, one launch (start us, length us, event | category | flops | bytes accessed | tf_op | source)
XLA Modules:
  0.0 552.2 jit_solution(12033018276002178137)
XLA Ops:
  15.8 6.7 %collective-permute-done.95.wd1 = bf16[3072,768]{1,0:T(8,128)(2,1)} collective-permute-done((bf16[3072,768]{1,0:T(8,128)(2,1)}, bf16[3072,768]{1,0:T(8,128)(2,1)}, u32[]{:S(2)}, u32[]{:S(2)}) %collective-permute-start.95) | collective-permute-done | bytes 4718624 | tf_op jit(solution)/shard_map/ppermute | solution.py:1067
  26.0 43.1 %layer_forward_all.1 = (f32[1024,384]{1,0:T(8,128)}, bf16[2,1024,384]{2,1,0:T(8,128)(2,1)}, bf16[1024,2304]{1,0:T(8,128)(2,1)}, bf16[1024,768]{1,0:T(8,128)(2,1)...) custom-call(s32[6]{0:T(128)} %copy-done.18, ...), custom_call_target="tpu_custom_call" | custom-call | flops 10000000000 | tf_op jit(solution)/shard_map/layer_forward_all/pallas_call | solution.py:482
  69.1 34.2 %ffn_back.2 = (f32[1024,768]{1,0:T(8,128)}, bf16[2,1536,768]{2,1,0:T(8,128)(2,1)}, bf16[2,1536,768]{2,1,0:T(8,128)(2,1)}, bf16[2,768,1536]{2,1,0:T(8,128)(2,1)},...) custom-call(s32[6]{0:T(128)} %copy-done.18, s32[6]{0:T(128)} %copy-done.19, s32[2]{0:T(128)} %assigned.13, s32[32]{0:T(128)} %lengths.13, ...), custom_call_target="tpu_custom_call" | custom-call | tf_op jit(solution)/shard_map/ffn_back/pallas_call | solution.py:711
  103.3 48.4 %attention_back.2 = (bf16[1024,768]{1,0:T(8,128)(2,1)}, bf16[2,784,1536]{2,1,0:T(8,128)(2,1)}, bf16[2,784,1536]{2,1,0:T(8,128)(2,1)}) custom-call(s32[6]{0:T(128)} %copy-done.18, s32[6]{0:T(128)} %copy-done.19, s32[2]{0:T(128)} %assigned.13, s32[32]{0:T(128)} %lengths.13, f32[1024,768]{1,0:T(8,128)} %get-tuple-element.199.res_hbm, ...), custom_call_target="tpu_custom_call" | custom-call | tf_op jit(solution)/shard_map/attention_back/pallas_call | solution.py:1027
  151.6 13.9 %ffn_back.3 = (f32[1024,768]{1,0:T(8,128)}, bf16[2,1536,768]{2,1,0:T(8,128)(2,1)}, bf16[2,1536,768]{2,1,0:T(8,128)(2,1)}, bf16[2,768,1536]{2,1,0:T(8,128)(2,1)},...) custom-call(s32[6]{0:T(128)} %copy-done.18, ...), custom_call_target="tpu_custom_call", output_to_operand_aliasing={{1}: (16, {}), {2}: (17, {}), {3}: (18, {}), {4}: (19, {})} | custom-call | tf_op jit(solution)/shard_map/ffn_back/pallas_call | solution.py:711
  165.5 4.6 attention_back.3
  170.1 381.9 %conditional.1 = (f32[1,3072,768]{2,1,0:T(8,128)}, f32[1,768,3072]{2,1,0:T(8,128)}, f32[1,768,768]{2,1,0:T(8,128)}, f32[1,768,2304]{2,1,0:T(8,128)}, f32[16,1536...) conditional(s32[]{:T(128)} %clamp.3, ...), branch_computations={%region_2.3_spmd, %region_3.4_spmd, %region_4.5_spmd} | conditional | flops 216000446464 | bytes 217032192 | solution.py:1490
  185.3 7.7 %collective-permute-done.got = bf16[2,1536,768]{2,1,0:T(8,128)(2,1)} collective-permute-done((bf16[2,1536,768]{2,1,0:T(8,128)(2,1)}, bf16[2,1536,768]{2,1,0:T(8,128)(2,1)}, u32[]{:S(2)}, u32[]{:S(2)}) %collective-permute-start) | collective-permute-done | bytes 4718624 | tf_op jit(solution)/shard_map/cond/branch_0_fun/ppermute | solution.py:1067
  193.0 3.8 half_sum.72.before
  199.7 3.8 half_sum.73.before
  203.5 17.1 %collective-permute-start.5 = (bf16[2,384,1536]{2,1,0:T(8,128)(2,1)}, bf16[2,384,1536]{2,1,0:T(8,128)(2,1)}, u32[]{:S(2)}, u32[]{:S(2)}) collective-permute-start(bf16[2,384,1536]{2,1,0:T(8,128)(2,1)} %half_sum.73.before), channel_id=1, source_target_pairs={{0,2},{1,3},{2,0},{3,1},{4,6},{5,7},{6,4},{7,5},{8,10},{9,11},{10,... | collective-permute-start | bytes 7077896 | tf_op jit(solution)/shard_map/cond/branch_0_fun/ppermute | solution.py:1072
  220.6 3.8 half_sum.74.before
  224.4 15.9 %collective-permute-start.4 = (bf16[2,400,1536]{2,1,0:T(8,128)(2,1)}, bf16[2,400,1536]{2,1,0:T(8,128)(2,1)}, u32[]{:S(2)}, u32[]{:S(2)}) collective-permute-start(bf16[2,400,1536]{2,1,0:T(8,128)(2,1)} %half_sum.74.before), channel_id=1, source_target_pairs={{0,4},{1,5},{2,6},{3,7},{4,0},{5,1},{6,2},{7,3},{8,12},{9,13},{10,... | collective-permute-start | bytes 7372808 | tf_op jit(solution)/shard_map/cond/branch_0_fun/ppermute | solution.py:1072
  240.3 3.8 half_sum.75.before.keep
  244.1 3.8 half_sum.76.before.keep
  247.9 3.8 half_sum.77.before.keep
  260.7 22.3 %collective-permute-start.7 = (bf16[2,384,768]{2,1,0:T(8,128)(2,1)}, bf16[2,384,768]{2,1,0:T(8,128)(2,1)}, u32[]{:S(2)}, u32[]{:S(2)}) collective-permute-start(bf16[2,384,768]{2,1,0:T(8,128)(2,1)} %half_sum.78.before), channel_id=1, source_target_pairs={{0,4},{1,5},{2,6},{3,7},{4,0},{5,1},{6,2},{7,3},{8,12},{9,13},{10,... | collective-permute-start | bytes 3538952 | tf_op jit(solution)/shard_map/cond/branch_0_fun/ppermute | solution.py:1072
  286.0 8.7 %collective-permute-done.4.got = bf16[2,400,1536]{2,1,0:T(8,128)(2,1)} collective-permute-done((bf16[2,400,1536]{2,1,0:T(8,128)(2,1)}, bf16[2,400,1536]{2,1,0:T(8,128)(2,1)}, u32[]{:S(2)}, u32[]{:S(2)}) %collective-permute-start.4) | collective-permute-done | bytes 2457632 | tf_op jit(solution)/shard_map/cond/branch_0_fun/ppermute | solution.py:1072
  306.2 13.3 %collective-permute-done.7.got = bf16[2,384,768]{2,1,0:T(8,128)(2,1)} collective-permute-done((bf16[2,384,768]{2,1,0:T(8,128)(2,1)}, bf16[2,384,768]{2,1,0:T(8,128)(2,1)}, u32[]{:S(2)}, u32[]{:S(2)}) %collective-permute-start.7) | collective-permute-done | bytes 1179680 | tf_op jit(solution)/shard_map/cond/branch_0_fun/ppermute | solution.py:1072
  335.7 14.8 %collective-permute-done.10.got = bf16[2,192,768]{2,1,0:T(8,128)(2,1)} collective-permute-done((bf16[2,192,768]{2,1,0:T(8,128)(2,1)}, bf16[2,192,768]{2,1,0:T(8,128)(2,1)}, u32[]{:S(2)}, u32[]{:S(2)}) %collective-permute-start.10) | collective-permute-done | bytes 589856 | tf_op jit(solution)/shard_map/cond/branch_0_fun/ppermute | solution.py:1072
  367.2 10.7 %collective-permute-done.17.two = bf16[2,48,1536]{2,1,0:T(8,128)(2,1)} collective-permute-done((bf16[2,48,1536]{2,1,0:T(8,128)(2,1)}, bf16[2,48,1536]{2,1,0:T(8,128)(2,1)}, u32[]{:S(2)}, u32[]{:S(2)}) %collective-permute-start.17) | collective-permute-done | bytes 294944 | tf_op jit(solution)/shard_map/cond/branch_0_fun/ppermute | solution.py:1072
  381.6 4.6 collective-permute-done.16.two
  396.9 30.2 %collective-permute-done.22.got = bf16[2,48,1536]{2,1,0:T(8,128)(2,1)} collective-permute-done((bf16[2,48,1536]{2,1,0:T(8,128)(2,1)}, bf16[2,48,1536]{2,1,0:T(8,128)(2,1)}, u32[]{:S(2)}, u32[]{:S(2)}) %collective-permute-start.22) | collective-permute-done | bytes 294944 | tf_op jit(solution)/shard_map/cond/branch_0_fun/ppermute | solution.py:1072
  429.1 4.5 collective-permute-done.20.got
  435.5 10.7 %collective-permute-done.19.got = bf16[2,192,768]{2,1,0:T(8,128)(2,1)} collective-permute-done((bf16[2,192,768]{2,1,0:T(8,128)(2,1)}, bf16[2,192,768]{2,1,0:T(8,128)(2,1)}, u32[]{:S(2)}, u32[]{:S(2)}) %collective-permute-start.19) | collective-permute-done | bytes 589856 | tf_op jit(solution)/shard_map/cond/branch_0_fun/ppermute | solution.py:1072
  448.3 10.5 %collective-permute-done.25.got = bf16[2,96,1536]{2,1,0:T(8,128)(2,1)} collective-permute-done((bf16[2,96,1536]{2,1,0:T(8,128)(2,1)}, bf16[2,96,1536]{2,1,0:T(8,128)(2,1)}, u32[]{:S(2)}, u32[]{:S(2)}) %collective-permute-start.25) | collective-permute-done | bytes 589856 | tf_op jit(solution)/shard_map/cond/branch_0_fun/ppermute | solution.py:1072
  467.7 16.3 %collective-permute-done.23.got = bf16[2,384,768]{2,1,0:T(8,128)(2,1)} collective-permute-done((bf16[2,384,768]{2,1,0:T(8,128)(2,1)}, bf16[2,384,768]{2,1,0:T(8,128)(2,1)}, u32[]{:S(2)}, u32[]{:S(2)}) %collective-permute-start.23) | collective-permute-done | bytes 1179680 | tf_op jit(solution)/shard_map/cond/branch_0_fun/ppermute | solution.py:1072
  496.0 3.8 place_rows.6.refs_0_
  499.8 3.7 place_cols.6.refs_0_
  507.2 32.9 %collective-permute-done.26.part = bf16[2,768,768]{2,1,0:T(8,128)(2,1)} collective-permute-done((bf16[2,768,768]{2,1,0:T(8,128)(2,1)}, bf16[2,768,768]{2,1,0:T(8,128)(2,1)}, u32[]{:S(2)}, u32[]{:S(2)}) %collective-permute-start.26) | collective-permute-done | bytes 2359328 | tf_op jit(solution)/shard_map/cond/branch_0_fun/ppermute | solution.py:1072
  540.2 3.8 place_rows.7.refs_1_
  544.2 3.7 place_cols.7.refs_2_
  (131 shorter events, 126.0 us)
Async XLA Ops:
  0.6 9.8 %collective-permute-start.97 = (bf16[768,2304]{1,0:T(8,128)(2,1)}, bf16[768,2304]{1,0:T(8,128)(2,1)}, u32[]{:S(2)}, u32[]{:S(2)}) collective-permute-start(bf16[768,2304]{1,0:T(8,128)(2,1)} %bitcast.69), channel_id=1, source_target_pairs={{0,16},{16,0},{1,17},{17,1},{2,18},{18,2},{3,19},{19,3},{4,20},{20... | collective-permute-start | bytes 10616840 | tf_op jit(solution)/shard_map/ppermute | solution.py:1067
  5.6 10.2 %collective-permute-start.94 = (bf16[768,3072]{1,0:T(8,128)(2,1)}, bf16[768,3072]{1,0:T(8,128)(2,1)}, u32[]{:S(2)}, u32[]{:S(2)}) collective-permute-start(bf16[768,3072]{1,0:T(8,128)(2,1)} %bitcast.59), channel_id=1, source_target_pairs={{0,16},{16,0},{1,17},{17,1},{2,18},{18,2},{3,19},{19,3},{4,20},{20... | collective-permute-start | bytes 14155784 | tf_op jit(solution)/shard_map/ppermute | solution.py:1067
  5.6 16.9 %collective-permute-start.95 = (bf16[3072,768]{1,0:T(8,128)(2,1)}, bf16[3072,768]{1,0:T(8,128)(2,1)}, u32[]{:S(2)}, u32[]{:S(2)}) collective-permute-start(bf16[3072,768]{1,0:T(8,128)(2,1)} %bitcast.64), channel_id=1, source_target_pairs={{0,16},{16,0},{1,17},{17,1},{2,18},{18,2},{3,19},{19,3},{4,20},{20... | collective-permute-start | bytes 14155784 | tf_op jit(solution)/shard_map/ppermute | solution.py:1067
  184.7 15.0 %collective-permute-start.2 = (bf16[2,768,1536]{2,1,0:T(8,128)(2,1)}, bf16[2,768,1536]{2,1,0:T(8,128)(2,1)}, u32[]{:S(2)}, u32[]{:S(2)}) collective-permute-start(bf16[2,768,1536]{2,1,0:T(8,128)(2,1)} %get-tuple-element.69), channel_id=1, source_target_pairs={{0,16},{16,0},{1,17},{17,1},{2,18},{18,2},{3,19},{19,3},{4,20},{20... | collective-permute-start | bytes 14155784 | tf_op jit(solution)/shard_map/cond/branch_0_fun/ppermute | solution.py:1067
  185.2 35.3 %collective-permute-start.1 = (bf16[2,784,1536]{2,1,0:T(8,128)(2,1)}, bf16[2,784,1536]{2,1,0:T(8,128)(2,1)}, u32[]{:S(2)}, u32[]{:S(2)}) collective-permute-start(bf16[2,784,1536]{2,1,0:T(8,128)(2,1)} %get-tuple-element.67), channel_id=1, source_target_pairs={{0,16},{16,0},{1,17},{17,1},{2,18},{18,2},{3,19},{19,3},{4,20},{20... | collective-permute-start | bytes 14450696 | tf_op jit(solution)/shard_map/cond/branch_0_fun/ppermute | solution.py:1067
  196.8 61.2 %collective-permute-start.3 = (bf16[2,768,768]{2,1,0:T(8,128)(2,1)}, bf16[2,768,768]{2,1,0:T(8,128)(2,1)}, u32[]{:S(2)}, u32[]{:S(2)}) collective-permute-start(bf16[2,768,768]{2,1,0:T(8,128)(2,1)} %half_sum.72.before), channel_id=1, source_target_pairs={{0,1},{1,0},{2,3},{3,2},{4,5},{5,4},{6,7},{7,6},{8,9},{9,8},{10,11... | collective-permute-start | bytes 7077896 | tf_op jit(solution)/shard_map/cond/branch_0_fun/ppermute | solution.py:1072
  203.5 79.5 %collective-permute-start.5 = (bf16[2,384,1536]{2,1,0:T(8,128)(2,1)}, bf16[2,384,1536]{2,1,0:T(8,128)(2,1)}, u32[]{:S(2)}, u32[]{:S(2)}) collective-permute-start(bf16[2,384,1536]{2,1,0:T(8,128)(2,1)} %half_sum.73.before), channel_id=1, source_target_pairs={{0,2},{1,3},{2,0},{3,1},{4,6},{5,7},{6,4},{7,5},{8,10},{9,11},{10,... | collective-permute-start | bytes 7077896 | tf_op jit(solution)/shard_map/cond/branch_0_fun/ppermute | solution.py:1072
  224.4 70.3 %collective-permute-start.4 = (bf16[2,400,1536]{2,1,0:T(8,128)(2,1)}, bf16[2,400,1536]{2,1,0:T(8,128)(2,1)}, u32[]{:S(2)}, u32[]{:S(2)}) collective-permute-start(bf16[2,400,1536]{2,1,0:T(8,128)(2,1)} %half_sum.74.before), channel_id=1, source_target_pairs={{0,4},{1,5},{2,6},{3,7},{4,0},{5,1},{6,2},{7,3},{8,12},{9,13},{10,... | collective-permute-start | bytes 7372808 | tf_op jit(solution)/shard_map/cond/branch_0_fun/ppermute | solution.py:1072
  240.3 11.5 %collective-permute-start.6 = (bf16[2,1024,384]{2,1,0:T(8,128)(2,1)}, bf16[2,1024,384]{2,1,0:T(8,128)(2,1)}, u32[]{:S(2)}, u32[]{:S(2)}) collective-permute-start(bf16[2,1024,384]{2,1,0:T(8,128)(2,1)} %get-tuple-element.70.before), channel_id=1, source_target_pairs={{0,16},{16,0},{1,17},{17,1},{2,18},{18,2},{3,19},{19,3},{4,20},{20... | collective-permute-start | bytes 4718600 | tf_op jit(solution)/shard_map/cond/branch_0_fun/ppermute | solution.py:1067
  260.7 58.8 %collective-permute-start.7 = (bf16[2,384,768]{2,1,0:T(8,128)(2,1)}, bf16[2,384,768]{2,1,0:T(8,128)(2,1)}, u32[]{:S(2)}, u32[]{:S(2)}) collective-permute-start(bf16[2,384,768]{2,1,0:T(8,128)(2,1)} %half_sum.78.before), channel_id=1, source_target_pairs={{0,4},{1,5},{2,6},{3,7},{4,0},{5,1},{6,2},{7,3},{8,12},{9,13},{10,... | collective-permute-start | bytes 3538952 | tf_op jit(solution)/shard_map/cond/branch_0_fun/ppermute | solution.py:1072
  285.7 36.1 %collective-permute-start.9 = (bf16[2,192,1536]{2,1,0:T(8,128)(2,1)}, bf16[2,192,1536]{2,1,0:T(8,128)(2,1)}, u32[]{:S(2)}, u32[]{:S(2)}) collective-permute-start(bf16[2,192,1536]{2,1,0:T(8,128)(2,1)} %half_sum.79.before), channel_id=1, source_target_pairs={{0,1},{1,0},{2,3},{3,2},{4,5},{5,4},{6,7},{7,6},{8,9},{9,8},{10,11... | collective-permute-start | bytes 3538952 | tf_op jit(solution)/shard_map/cond/branch_0_fun/ppermute | solution.py:1072
  297.5 29.5 %collective-permute-start.8 = (bf16[2,208,1536]{2,1,0:T(8,128)(2,1)}, bf16[2,208,1536]{2,1,0:T(8,128)(2,1)}, u32[]{:S(2)}, u32[]{:S(2)}) collective-permute-start(bf16[2,208,1536]{2,1,0:T(8,128)(2,1)} %half_sum.80.before), channel_id=1, source_target_pairs={{0,2},{1,3},{2,0},{3,1},{4,6},{5,7},{6,4},{7,5},{8,10},{9,11},{10,... | collective-permute-start | bytes 3833864 | tf_op jit(solution)/shard_map/cond/branch_0_fun/ppermute | solution.py:1072
  321.7 28.9 %collective-permute-start.10 = (bf16[2,192,768]{2,1,0:T(8,128)(2,1)}, bf16[2,192,768]{2,1,0:T(8,128)(2,1)}, u32[]{:S(2)}, u32[]{:S(2)}) collective-permute-start(bf16[2,192,768]{2,1,0:T(8,128)(2,1)} %half_sum.84.before), channel_id=1, source_target_pairs={{0,8},{1,9},{2,10},{3,11},{4,12},{5,13},{6,14},{7,15},{8,0},{9,1},... | collective-permute-start | bytes 1769480 | tf_op jit(solution)/shard_map/cond/branch_0_fun/ppermute | solution.py:1072
  323.9 28.7 %collective-permute-start.12 = (bf16[2,96,1536]{2,1,0:T(8,128)(2,1)}, bf16[2,96,1536]{2,1,0:T(8,128)(2,1)}, u32[]{:S(2)}, u32[]{:S(2)}) collective-permute-start(bf16[2,96,1536]{2,1,0:T(8,128)(2,1)} %half_sum.85.before), channel_id=1, source_target_pairs={{0,4},{1,5},{2,6},{3,7},{4,0},{5,1},{6,2},{7,3},{8,12},{9,13},{10,... | collective-permute-start | bytes 1769480 | tf_op jit(solution)/shard_map/cond/branch_0_fun/ppermute | solution.py:1072
  329.1 26.0 %collective-permute-start.11 = (bf16[2,112,1536]{2,1,0:T(8,128)(2,1)}, bf16[2,112,1536]{2,1,0:T(8,128)(2,1)}, u32[]{:S(2)}, u32[]{:S(2)}) collective-permute-start(bf16[2,112,1536]{2,1,0:T(8,128)(2,1)} %half_sum.86.before), channel_id=1, source_target_pairs={{0,1},{1,0},{2,3},{3,2},{4,5},{5,4},{6,7},{7,6},{8,9},{9,8},{10,11... | collective-permute-start | bytes 2064392 | tf_op jit(solution)/shard_map/cond/branch_0_fun/ppermute | solution.py:1072
  352.5 12.9 %collective-permute-start.13 = (bf16[2,96,768]{2,1,0:T(8,128)(2,1)}, bf16[2,96,768]{2,1,0:T(8,128)(2,1)}, u32[]{:S(2)}, u32[]{:S(2)}) collective-permute-start(bf16[2,96,768]{2,1,0:T(8,128)(2,1)} %half_sum.90.before), channel_id=1, source_target_pairs={{0,2},{1,3},{2,0},{3,1},{4,6},{5,7},{6,4},{7,5},{8,10},{9,11},{10,... | collective-permute-start | bytes 884744 | tf_op jit(solution)/shard_map/cond/branch_0_fun/ppermute | solution.py:1072
  354.5 23.4 %collective-permute-start.17 = (bf16[2,48,1536]{2,1,0:T(8,128)(2,1)}, bf16[2,48,1536]{2,1,0:T(8,128)(2,1)}, u32[]{:S(2)}, u32[]{:S(2)}) collective-permute-start(bf16[2,48,1536]{2,1,0:T(8,128)(2,1)} %half_sum.91.before), channel_id=1, source_target_pairs={{0,8},{1,9},{2,10},{3,11},{4,12},{5,13},{6,14},{7,15},{8,0},{9,1},... | collective-permute-start | bytes 884744 | tf_op jit(solution)/shard_map/cond/branch_0_fun/ppermute | solution.py:1072
  357.1 29.1 %collective-permute-start.16 = (bf16[2,64,1536]{2,1,0:T(8,128)(2,1)}, bf16[2,64,1536]{2,1,0:T(8,128)(2,1)}, u32[]{:S(2)}, u32[]{:S(2)}) collective-permute-start(bf16[2,64,1536]{2,1,0:T(8,128)(2,1)} %half_sum.92.before), channel_id=1, source_target_pairs={{0,8},{1,9},{2,10},{3,11},{4,12},{5,13},{6,14},{7,15},{8,0},{9,1},... | collective-permute-start | bytes 1179656 | tf_op jit(solution)/shard_map/cond/branch_0_fun/ppermute | solution.py:1072
  367.2 12.5 %collective-permute-start.14 = (bf16[1,96,768]{2,1,0:T(8,128)(2,1)}, bf16[1,96,768]{2,1,0:T(8,128)(2,1)S(1)}, u32[]{:S(2)}, u32[]{:S(2)}) collective-permute-start(bf16[1,96,768]{2,1,0:T(8,128)(2,1)} %get-tuple-element.74.before), channel_id=1, source_target_pairs={{0,16},{16,0},{1,17},{17,1},{2,18},{18,2},{3,19},{19,3},{4,20},{20... | collective-permute-start | bytes 442376 | tf_op jit(solution)/shard_map/cond/branch_0_fun/ppermute | solution.py:1067
  379.7 10.5 %collective-permute-start.21 = (bf16[1,48,1536]{2,1,0:T(8,128)(2,1)}, bf16[1,48,1536]{2,1,0:T(8,128)(2,1)S(1)}, u32[]{:S(2)}, u32[]{:S(2)}) collective-permute-start(bf16[1,48,1536]{2,1,0:T(8,128)(2,1)} %get-tuple-element.75.before), channel_id=1, source_target_pairs={{0,16},{16,0},{1,17},{17,1},{2,18},{18,2},{3,19},{19,3},{4,20},{20... | collective-permute-start | bytes 442376 | tf_op jit(solution)/shard_map/cond/branch_0_fun/ppermute | solution.py:1067
  379.9 15.1 %collective-permute-start.15 = (bf16[2,96,768]{2,1,0:T(8,128)(2,1)S(1)}, bf16[2,96,768]{2,1,0:T(8,128)(2,1)}, u32[]{:S(2)}, u32[]{:S(2)}) collective-permute-start(bf16[2,96,768]{2,1,0:T(8,128)(2,1)S(1)} %broadcast_select_fusion.2.part), channel_id=1, source_target_pairs={{0,2},{1,3},{2,0},{3,1},{4,6},{5,7},{6,4},{7,5},{8,10},{9,11},{10,... | collective-permute-start | bytes 884744 | tf_op jit(solution)/shard_map/cond/branch_0_fun/ppermute | solution.py:1072
  392.1 35.1 %collective-permute-start.22 = (bf16[2,48,1536]{2,1,0:T(8,128)(2,1)}, bf16[2,48,1536]{2,1,0:T(8,128)(2,1)}, u32[]{:S(2)}, u32[]{:S(2)}) collective-permute-start(bf16[2,48,1536]{2,1,0:T(8,128)(2,1)} %get-tuple-element.255.part), channel_id=1, source_target_pairs={{0,8},{1,9},{2,10},{3,11},{4,12},{5,13},{6,14},{7,15},{8,0},{9,1},... | collective-permute-start | bytes 884744 | tf_op jit(solution)/shard_map/cond/branch_0_fun/ppermute | solution.py:1072
  392.1 41.5 %collective-permute-start.20 = (bf16[2,48,1536]{2,1,0:T(8,128)(2,1)}, bf16[2,48,1536]{2,1,0:T(8,128)(2,1)}, u32[]{:S(2)}, u32[]{:S(2)}) collective-permute-start(bf16[2,48,1536]{2,1,0:T(8,128)(2,1)} %get-tuple-element.256.before.part), channel_id=1, source_target_pairs={{0,8},{1,9},{2,10},{3,11},{4,12},{5,13},{6,14},{7,15},{8,0},{9,1},... | collective-permute-start | bytes 884744 | tf_op jit(solution)/shard_map/cond/branch_0_fun/ppermute | solution.py:1072
  396.9 49.4 %collective-permute-start.19 = (bf16[2,192,768]{2,1,0:T(8,128)(2,1)}, bf16[2,192,768]{2,1,0:T(8,128)(2,1)}, u32[]{:S(2)}, u32[]{:S(2)}) collective-permute-start(bf16[2,192,768]{2,1,0:T(8,128)(2,1)} %join.27.before.part), channel_id=1, source_target_pairs={{0,8},{1,9},{2,10},{3,11},{4,12},{5,13},{6,14},{7,15},{8,0},{9,1},... | collective-permute-start | bytes 1769480 | tf_op jit(solution)/shard_map/cond/branch_0_fun/ppermute | solution.py:1072
  429.0 29.8 %collective-permute-start.25 = (bf16[2,96,1536]{2,1,0:T(8,128)(2,1)}, bf16[2,96,1536]{2,1,0:T(8,128)(2,1)}, u32[]{:S(2)}, u32[]{:S(2)}) collective-permute-start(bf16[2,96,1536]{2,1,0:T(8,128)(2,1)} %join.28.before.part), channel_id=1, source_target_pairs={{0,4},{1,5},{2,6},{3,7},{4,0},{5,1},{6,2},{7,3},{8,12},{9,13},{10,... | collective-permute-start | bytes 1769480 | tf_op jit(solution)/shard_map/cond/branch_0_fun/ppermute | solution.py:1072
  435.5 25.5 %collective-permute-start.24 = (bf16[2,96,1536]{2,1,0:T(8,128)(2,1)}, bf16[2,96,1536]{2,1,0:T(8,128)(2,1)}, u32[]{:S(2)}, u32[]{:S(2)}) collective-permute-start(bf16[2,96,1536]{2,1,0:T(8,128)(2,1)} %join.29.before.part), channel_id=1, source_target_pairs={{0,1},{1,0},{2,3},{3,2},{4,5},{5,4},{6,7},{7,6},{8,9},{9,8},{10,11... | collective-permute-start | bytes 1769480 | tf_op jit(solution)/shard_map/cond/branch_0_fun/ppermute | solution.py:1072
  448.2 35.8 %collective-permute-start.23 = (bf16[2,384,768]{2,1,0:T(8,128)(2,1)}, bf16[2,384,768]{2,1,0:T(8,128)(2,1)}, u32[]{:S(2)}, u32[]{:S(2)}) collective-permute-start(bf16[2,384,768]{2,1,0:T(8,128)(2,1)} %join.30.before.part), channel_id=1, source_target_pairs={{0,4},{1,5},{2,6},{3,7},{4,0},{5,1},{6,2},{7,3},{8,12},{9,13},{10,... | collective-permute-start | bytes 3538952 | tf_op jit(solution)/shard_map/cond/branch_0_fun/ppermute | solution.py:1072
  460.9 28.2 %collective-permute-start.28 = (bf16[2,192,1536]{2,1,0:T(8,128)(2,1)}, bf16[2,192,1536]{2,1,0:T(8,128)(2,1)}, u32[]{:S(2)}, u32[]{:S(2)}) collective-permute-start(bf16[2,192,1536]{2,1,0:T(8,128)(2,1)} %join.31.before.part), channel_id=1, source_target_pairs={{0,1},{1,0},{2,3},{3,2},{4,5},{5,4},{6,7},{7,6},{8,9},{9,8},{10,11... | collective-permute-start | bytes 3538952 | tf_op jit(solution)/shard_map/cond/branch_0_fun/ppermute | solution.py:1072
  463.0 30.4 %collective-permute-start.27 = (bf16[2,192,1536]{2,1,0:T(8,128)(2,1)}, bf16[2,192,1536]{2,1,0:T(8,128)(2,1)}, u32[]{:S(2)}, u32[]{:S(2)}) collective-permute-start(bf16[2,192,1536]{2,1,0:T(8,128)(2,1)} %join.32.before.part), channel_id=1, source_target_pairs={{0,2},{1,3},{2,0},{3,1},{4,6},{5,7},{6,4},{7,5},{8,10},{9,11},{10,... | collective-permute-start | bytes 3538952 | tf_op jit(solution)/shard_map/cond/branch_0_fun/ppermute | solution.py:1072
  486.6 53.6 %collective-permute-start.26 = (bf16[2,768,768]{2,1,0:T(8,128)(2,1)}, bf16[2,768,768]{2,1,0:T(8,128)(2,1)}, u32[]{:S(2)}, u32[]{:S(2)}) collective-permute-start(bf16[2,768,768]{2,1,0:T(8,128)(2,1)} %join.33.before.part), channel_id=1, source_target_pairs={{0,1},{1,0},{2,3},{3,2},{4,5},{5,4},{6,7},{7,6},{8,9},{9,8},{10,11... | collective-permute-start | bytes 7077896 | tf_op jit(solution)/shard_map/cond/branch_0_fun/ppermute | solution.py:1072
  491.6 52.6 %collective-permute-start.29 = (bf16[2,384,1536]{2,1,0:T(8,128)(2,1)}, bf16[2,384,1536]{2,1,0:T(8,128)(2,1)}, u32[]{:S(2)}, u32[]{:S(2)}) collective-permute-start(bf16[2,384,1536]{2,1,0:T(8,128)(2,1)} %join.34.before.part), channel_id=1, source_target_pairs={{0,2},{1,3},{2,0},{3,1},{4,6},{5,7},{6,4},{7,5},{8,10},{9,11},{10,... | collective-permute-start | bytes 7077896 | tf_op jit(solution)/shard_map/cond/branch_0_fun/ppermute | solution.py:1072
  495.9 52.3 %collective-permute-start.30 = (bf16[2,384,1536]{2,1,0:T(8,128)(2,1)}, bf16[2,384,1536]{2,1,0:T(8,128)(2,1)}, u32[]{:S(2)}, u32[]{:S(2)}) collective-permute-start(bf16[2,384,1536]{2,1,0:T(8,128)(2,1)} %join.35.refs_0_.part), channel_id=1, source_target_pairs={{0,4},{1,5},{2,6},{3,7},{4,0},{5,1},{6,2},{7,3},{8,12},{9,13},{10,... | collective-permute-start | bytes 7077896 | tf_op jit(solution)/shard_map/cond/branch_0_fun/ppermute | solution.py:1072
  (13 other events, 73.3 us)
